TPU v7x, 256 devices: a whole 4x4x8 slice. The times are simulated.
256 devices in a mesh: ka: 4 (over x), pair: 16 (over z, core), aux: 4 (over y).
Axes of the slice: x: 4, y: 4, z: 8, core: 2. Of those that a mesh axis runs over, the one named last changes fastest.
Arguments:
- kpoint_grid: int32 [16, 3], P(('ka', 'aux')), may hold values from 0 to 3, as said below
- image_shift: int32 [3, 4, 6144], P(None, None, 'pair'), may hold values from -2 to 2
- density_k: bfloat16 [16, 4, 6144, 2, 1024], P(('ka', 'aux'), None, 'pair'), may hold values from -24 to 24
- coefficients: bfloat16 [2048, 256, 1024], P(('ka', 'pair'), 'aux'), may hold values from -1 to 1
- coulomb: float32 [24576, 256], P(('ka', 'pair'), 'aux'), may hold values from 0.002 to 0.08
- send_rows: int32 [64, 64, 32], P(('ka', 'pair')), may hold values from -1 to 383, as said below
- source_index: int32 [24576, 16], P(('ka', 'pair')), may hold values from 0 to 2431
- list_length: int32 [24576], P(('ka', 'pair')), may hold values from 1 to 16
Outputs:
- exchange_blocks: bfloat16 [24576, 1024], P(('ka', 'pair'), 'aux')
Inputs may be any that keep to these rules, and one draw needn't show every extreme that they name: `kpoint_grid`: the rows are the 16 points of the 4 x 2 x 2 grid, each once, in an order drawn from the seed. `send_rows`: each entry is a row of the sending slab (below 384) or -1 for an empty slot; filled slots come first; each slab fills all 32 slots to the slab after it, cyclically.
All inputs are finite; a program needn't handle non-finite values.
Results may differ from a plain program's by a relative error of at most 0.025.
Values may be sent and summed in bfloat16 or wider, within the bound.
No kernel may reach another device: no remote copies, remote signals or barrier semaphores. Data moves between devices by JAX's collectives and lax.ppermute only.
A program may use at most 128 MiB of HBM per device.

v0:
```python
import math

import jax
import jax.numpy as jnp
from jax import lax
from jax.sharding import PartitionSpec as P

NB = 32
NK = 16


def gather_rows(slab, rows):
    picked = jnp.take(slab, jnp.maximum(rows, 0), axis=0)
    return jnp.where((rows >= 0)[..., None], picked, jnp.zeros((), slab.dtype))


def move_blocks(blocks):
    return lax.all_to_all(blocks, ("ka", "pair"), split_axis=0, concat_axis=0, tiled=True)


def atom_group(items):
    coeff, ymat, weights = items
    inner = jnp.einsum("apmn,atnl->atpml", coeff, ymat, preferred_element_type=jnp.float32)
    inner = (inner * weights[..., None, None]).astype(jnp.bfloat16)
    return jnp.einsum("atpml,apkl->atmk", inner, coeff, preferred_element_type=jnp.float32)


def shards(
    kpoint_grid, image_shift, density_k, coefficients, coulomb, send_rows, source_index, list_length
):
    width = density_k.shape[-1]
    kvec = kpoint_grid[0]
    turns = jnp.mod(
        kvec[0] * image_shift[0] * (NK // 4)
        + kvec[1] * image_shift[1] * (NK // 2)
        + kvec[2] * image_shift[2] * (NK // 2),
        NK,
    )
    angle = turns.astype(jnp.float32) * (2.0 * math.pi / NK)
    block = density_k[0]
    term = (
        block[:, :, 0].astype(jnp.float32) * jnp.cos(angle)[..., None]
        + block[:, :, 1].astype(jnp.float32) * jnp.sin(angle)[..., None]
    ) / NK
    term = term.reshape(-1, width)
    partial_sum = lax.psum_scatter(term.astype(jnp.bfloat16), "ka", scatter_dimension=0, tiled=True)
    slab = lax.psum(partial_sum, "aux")
    rows_out = send_rows[0]
    received = move_blocks(gather_rows(slab, rows_out))
    pool = jnp.concatenate([slab, received.reshape(-1, width)], 0)
    picked = jnp.take(pool, source_index, axis=0)
    mask = (jnp.arange(source_index.shape[1])[None, :] < list_length[:, None]).astype(jnp.bfloat16)
    summed = jnp.einsum("tg,tgn->tn", mask, picked, preferred_element_type=jnp.float32).astype(
        jnp.bfloat16
    )
    target_rows = summed.shape[0]
    atoms = coefficients.shape[0]
    aux_local = coefficients.shape[1]
    pairs_atom = target_rows // atoms
    group = math.gcd(atoms, 4)
    coeff = coefficients.reshape(atoms // group, group, aux_local, NB, NB)
    ymat = summed.reshape(atoms // group, group, pairs_atom, NB, NB)
    weights = coulomb.reshape(atoms // group, group, pairs_atom, aux_local)
    partial_blocks = lax.map(atom_group, (coeff, ymat, weights)).reshape(target_rows, width)
    return lax.psum_scatter(
        partial_blocks.astype(jnp.bfloat16), "aux", scatter_dimension=1, tiled=True
    )


def solution(mesh):
    placed = (
        P(("ka", "aux"), None),
        P(None, None, "pair"),
        P(("ka", "aux"), None, "pair", None, None),
        P(("ka", "pair"), "aux", None),
        P(("ka", "pair"), "aux"),
        P(("ka", "pair"), None, None),
        P(("ka", "pair"), None),
        P(("ka", "pair")),
    )
    return jax.shard_map(
        shards, mesh=mesh, in_specs=placed, out_specs=P(("ka", "pair"), "aux"), check_vma=False
    )
```

profile of v0, /device:TPU:2, one launch (start us, length us, event | category | flops | bytes accessed | tf_op | source)
XLA Modules:
  0.0 576.4 jit_solution(8724602714371758320)
XLA Ops:
  6.5 1.4 fusion.33
  7.9 2.6 multiply_add_fusion
  10.6 12.8 %slice_convert_fusion.1 = (f32[4,384,1,1024]{3,2,1,0:T(1,128)S(1)}, f32[4,384,1,1024]{3,2,1,0:T(1,128)S(1)}) fusion(bf16[4,384,2,1024]{3,2,1,0:T(2,128)(2,1)} %bitcast.73), kind=kLoop, calls=%fused_computation.23 | loop fusion | flops 3145728 | bytes 18874368 | tf_op jit(solution)/shard_map/convert_element_type | solution.py:42
  23.3 1.5 copy.29
  24.9 1.5 copy.30
  26.4 2.4 fusion.23
  28.9 42.6 %reduce-scatter.3.cloned.1.call-done = bf16[384,1024]{1,0:T(8,128)(2,1)} async-done(((bf16[1536,1024]{1,0:T(8,128)(2,1)}), bf16[384,1024]{1,0:T(8,128)(2,1)}) %reduce-scatter.3.cloned.1.call-update) | async-done | bytes 786448 | tf_op jit(solution)/shard_map/reduce_scatter | solution.py:46
  71.9 52.5 %all-reduce.2.cloned.1.call-done = bf16[384,1024]{1,0:T(8,128)(2,1)} async-done(((bf16[384,1024]{1,0:T(8,128)(2,1)}), bf16[384,1024]{1,0:T(8,128)(2,1)}) %all-reduce.2.cloned.1.call-update) | async-done | bytes 786448 | tf_op jit(solution)/shard_map/psum | solution.py:47
  124.4 12.2 %gather_fusion = bf16[2048,1024]{1,0:T(8,128)(2,1)} fusion(bf16[384,1024]{1,0:T(8,128)(2,1)} %all-reduce.2.cloned.1.call-done, s32[2048]{0:T(1024)S(1)} %broadcast_clamp_fusion.1), kind=kCustom, calls=%fused_computation | custom fusion | bytes 8396800 | tf_op jit(solution)/shard_map/jit(_take)/gather | solution.py:13
  136.6 3.9 select_select_fusion
  140.5 10.9 %all-to-all-start = ((bf16[64,32,1024]{2,1,0:T(8,128)(2,1)}), bf16[64,32,1024]{2,1,0:T(8,128)(2,1)}, u32[]{:S(2)}, u32[]{:S(2)}) async-start(bf16[64,32,1024]{2,1,0:T(8,128)(2,1)} %select_select_fusion), calls=%async_computation.1 | async-start | bytes 8388608 | tf_op jit(solution)/shard_map/all_to_all | solution.py:18
  152.2 8.5 %copy.18 = bf16[32,64,1024]{1,2,0:T(8,128)(2,1)} copy(bf16[32,64,1024]{2,1,0:T(8,128)(2,1)} %param.13) | data formatting | bytes 8388608 | tf_op args[3]
  161.0 85.3 %all-to-all-done = bf16[64,32,1024]{2,1,0:T(8,128)(2,1)} async-done(((bf16[64,32,1024]{2,1,0:T(8,128)(2,1)}), bf16[64,32,1024]{2,1,0:T(8,128)(2,1)}, u32[]{:S(2)}, u32[]{:S(2)}) %all-to-all-start) | async-done | bytes 4194336 | tf_op jit(solution)/shard_map/all_to_all | solution.py:18
  246.3 4.9 pad_maximum_fusion
  251.2 33.9 %gather_fusion.1 = bf16[6144,1024]{1,0:T(8,128)(2,1)} fusion(bf16[2432,1024]{1,0:T(8,128)(2,1)} %pad_maximum_fusion, s32[6144]{0:T(1024)S(1)} %broadcast_clamp_fusion), kind=kCustom, calls=%fused_computation.1 | custom fusion | bytes 25190400 | tf_op jit(solution)/shard_map/jit(_take)/gather | solution.py:51
  285.1 5.9 %fusion.18 = bf16[384,1,1024]{2,1,0:T(2,128)(2,1)S(1)} fusion(bf16[384,16,1024]{2,1,0:T(8,128)(2,1)} %bitcast.76, pred[384,16]{1,0:T(8,128)(4,1)S(1)} %copy.13, pred[384,16,1]{1,0,2:T(32,128)(4,1)S(1)} %fusion.26), kind=kOutput, calls=%fused_computation.19 | convolution fusion | flops 18874368 | bytes 13381632 | tf_op jit(solution)/shard_map/tg,tgn->tn/dot_general | solution.py:53
  291.0 1.2 copy.52
  292.1 3.8 reshape.127
  295.9 246.2 %while.10 = (s32[]{:T(128)}, bf16[8,4,12,32,32]{4,3,2,1,0:T(8,128)(2,1)}, bf16[8,4,12,32,32]{4,3,2,1,0:T(8,128)(2,1)S(1)}, bf16[8,4,64,32,32]{2,4,3,1,0:T(8,128)(2,1)}, f32[8,4,12,64]{3,2,1,0:T(8,128)S(1)}, /*index=5*/s32[]{:T(128)}) while((s32[]{:T(128)}, bf16[8,4,12,32,32]{4,3,2,1,0:T(8,128)(2,1)}, ...), condition=%wide.region_3.4_spmd, body=%wide.region_2.3_spmd.sunk | while | flops 408944640 | bytes 42635856 | solution.py:64
  296.1 1.3 constant_dynamic-slice_fusion.2
  297.4 0.4 copy.60
  297.8 10.1 %fusion.44 = f32[4,12,32,64,32]{3,2,4,1,0:T(8,128)} fusion(bf16[4,64,32,32,1]{1,2,3,0,4:T(8,128)(2,1)S(1)} %bitcast.72, bf16[8,4,12,32,32]{4,3,2,1,0:T(8,128)(2,1)S(1)} %get-tuple-element.102, s32[]{:T(128)} %get-tuple-element.94), kind=kOutput, calls=%fused_computation.10.clone.1 | convolution fusion | flops 201326592 | bytes 14024708 | tf_op jit(solution)/shard_map/while/body/eval_jaxpr/apmn,atnl->atpml/dot_general | solution.py:23
  307.9 18.9 %fusion.45 = bf16[8,4,12,32,32]{4,3,2,1,0:T(8,128)(2,1)} fusion(bf16[8,4,12,32,32]{4,3,2,1,0:T(8,128)(2,1)} %get-tuple-element.95, s32[]{:T(128)} %get-tuple-element.94, f32[4,12,32,64,32]{3,2,4,1,0:T(8,128)} %fusion.44, f32[4,12,64]{2,1,0:T(8,128)S(1)} %dynamic-slice_bitcast_fusion.2, bf16[1,4,64,32,32]{2,4,3,1,0:T(8,128)(2,1)S(1)} %constant_dynamic-slice_fusion.2), kind=kOutput, calls=%fused_computation.8.clone.1 | convolution fusion | flops 207618048 | bytes 26489344 | tf_op jit(solution)/shard_map/while/body/eval_jaxpr/atpml,apkl->atmk/dot_general | solution.py:25
  326.9 1.3 constant_dynamic-slice_fusion.2
  328.2 0.4 copy.60
  328.6 10.1 %fusion.44 = f32[4,12,32,64,32]{3,2,4,1,0:T(8,128)} fusion(bf16[4,64,32,32,1]{1,2,3,0,4:T(8,128)(2,1)S(1)} %bitcast.72, bf16[8,4,12,32,32]{4,3,2,1,0:T(8,128)(2,1)S(1)} %get-tuple-element.102, s32[]{:T(128)} %get-tuple-element.94), kind=kOutput, calls=%fused_computation.10.clone.1 | convolution fusion | flops 201326592 | bytes 14024708 | tf_op jit(solution)/shard_map/while/body/eval_jaxpr/apmn,atnl->atpml/dot_general | solution.py:23
  338.7 18.9 %fusion.45 = bf16[8,4,12,32,32]{4,3,2,1,0:T(8,128)(2,1)} fusion(bf16[8,4,12,32,32]{4,3,2,1,0:T(8,128)(2,1)} %get-tuple-element.95, s32[]{:T(128)} %get-tuple-element.94, f32[4,12,32,64,32]{3,2,4,1,0:T(8,128)} %fusion.44, f32[4,12,64]{2,1,0:T(8,128)S(1)} %dynamic-slice_bitcast_fusion.2, bf16[1,4,64,32,32]{2,4,3,1,0:T(8,128)(2,1)S(1)} %constant_dynamic-slice_fusion.2), kind=kOutput, calls=%fused_computation.8.clone.1 | convolution fusion | flops 207618048 | bytes 26489344 | tf_op jit(solution)/shard_map/while/body/eval_jaxpr/atpml,apkl->atmk/dot_general | solution.py:25
  357.6 1.3 constant_dynamic-slice_fusion.2
  358.9 0.4 copy.60
  359.3 10.1 %fusion.44 = f32[4,12,32,64,32]{3,2,4,1,0:T(8,128)} fusion(bf16[4,64,32,32,1]{1,2,3,0,4:T(8,128)(2,1)S(1)} %bitcast.72, bf16[8,4,12,32,32]{4,3,2,1,0:T(8,128)(2,1)S(1)} %get-tuple-element.102, s32[]{:T(128)} %get-tuple-element.94), kind=kOutput, calls=%fused_computation.10.clone.1 | convolution fusion | flops 201326592 | bytes 14024708 | tf_op jit(solution)/shard_map/while/body/eval_jaxpr/apmn,atnl->atpml/dot_general | solution.py:23
  369.4 18.9 %fusion.45 = bf16[8,4,12,32,32]{4,3,2,1,0:T(8,128)(2,1)} fusion(bf16[8,4,12,32,32]{4,3,2,1,0:T(8,128)(2,1)} %get-tuple-element.95, s32[]{:T(128)} %get-tuple-element.94, f32[4,12,32,64,32]{3,2,4,1,0:T(8,128)} %fusion.44, f32[4,12,64]{2,1,0:T(8,128)S(1)} %dynamic-slice_bitcast_fusion.2, bf16[1,4,64,32,32]{2,4,3,1,0:T(8,128)(2,1)S(1)} %constant_dynamic-slice_fusion.2), kind=kOutput, calls=%fused_computation.8.clone.1 | convolution fusion | flops 207618048 | bytes 26489344 | tf_op jit(solution)/shard_map/while/body/eval_jaxpr/atpml,apkl->atmk/dot_general | solution.py:25
  388.4 1.3 constant_dynamic-slice_fusion.2
  390.1 10.1 %fusion.44 = f32[4,12,32,64,32]{3,2,4,1,0:T(8,128)} fusion(bf16[4,64,32,32,1]{1,2,3,0,4:T(8,128)(2,1)S(1)} %bitcast.72, bf16[8,4,12,32,32]{4,3,2,1,0:T(8,128)(2,1)S(1)} %get-tuple-element.102, s32[]{:T(128)} %get-tuple-element.94), kind=kOutput, calls=%fused_computation.10.clone.1 | convolution fusion | flops 201326592 | bytes 14024708 | tf_op jit(solution)/shard_map/while/body/eval_jaxpr/apmn,atnl->atpml/dot_general | solution.py:23
  400.2 18.9 %fusion.45 = bf16[8,4,12,32,32]{4,3,2,1,0:T(8,128)(2,1)} fusion(bf16[8,4,12,32,32]{4,3,2,1,0:T(8,128)(2,1)} %get-tuple-element.95, s32[]{:T(128)} %get-tuple-element.94, f32[4,12,32,64,32]{3,2,4,1,0:T(8,128)} %fusion.44, f32[4,12,64]{2,1,0:T(8,128)S(1)} %dynamic-slice_bitcast_fusion.2, bf16[1,4,64,32,32]{2,4,3,1,0:T(8,128)(2,1)S(1)} %constant_dynamic-slice_fusion.2), kind=kOutput, calls=%fused_computation.8.clone.1 | convolution fusion | flops 207618048 | bytes 26489344 | tf_op jit(solution)/shard_map/while/body/eval_jaxpr/atpml,apkl->atmk/dot_general | solution.py:25
  419.1 1.3 constant_dynamic-slice_fusion.2
  420.8 10.1 %fusion.44 = f32[4,12,32,64,32]{3,2,4,1,0:T(8,128)} fusion(bf16[4,64,32,32,1]{1,2,3,0,4:T(8,128)(2,1)S(1)} %bitcast.72, bf16[8,4,12,32,32]{4,3,2,1,0:T(8,128)(2,1)S(1)} %get-tuple-element.102, s32[]{:T(128)} %get-tuple-element.94), kind=kOutput, calls=%fused_computation.10.clone.1 | convolution fusion | flops 201326592 | bytes 14024708 | tf_op jit(solution)/shard_map/while/body/eval_jaxpr/apmn,atnl->atpml/dot_general | solution.py:23
  430.9 18.9 %fusion.45 = bf16[8,4,12,32,32]{4,3,2,1,0:T(8,128)(2,1)} fusion(bf16[8,4,12,32,32]{4,3,2,1,0:T(8,128)(2,1)} %get-tuple-element.95, s32[]{:T(128)} %get-tuple-element.94, f32[4,12,32,64,32]{3,2,4,1,0:T(8,128)} %fusion.44, f32[4,12,64]{2,1,0:T(8,128)S(1)} %dynamic-slice_bitcast_fusion.2, bf16[1,4,64,32,32]{2,4,3,1,0:T(8,128)(2,1)S(1)} %constant_dynamic-slice_fusion.2), kind=kOutput, calls=%fused_computation.8.clone.1 | convolution fusion | flops 207618048 | bytes 26489344 | tf_op jit(solution)/shard_map/while/body/eval_jaxpr/atpml,apkl->atmk/dot_general | solution.py:25
  449.8 1.3 constant_dynamic-slice_fusion.2
  451.6 10.1 %fusion.44 = f32[4,12,32,64,32]{3,2,4,1,0:T(8,128)} fusion(bf16[4,64,32,32,1]{1,2,3,0,4:T(8,128)(2,1)S(1)} %bitcast.72, bf16[8,4,12,32,32]{4,3,2,1,0:T(8,128)(2,1)S(1)} %get-tuple-element.102, s32[]{:T(128)} %get-tuple-element.94), kind=kOutput, calls=%fused_computation.10.clone.1 | convolution fusion | flops 201326592 | bytes 14024708 | tf_op jit(solution)/shard_map/while/body/eval_jaxpr/apmn,atnl->atpml/dot_general | solution.py:23
  461.7 19.0 %fusion.45 = bf16[8,4,12,32,32]{4,3,2,1,0:T(8,128)(2,1)} fusion(bf16[8,4,12,32,32]{4,3,2,1,0:T(8,128)(2,1)} %get-tuple-element.95, s32[]{:T(128)} %get-tuple-element.94, f32[4,12,32,64,32]{3,2,4,1,0:T(8,128)} %fusion.44, f32[4,12,64]{2,1,0:T(8,128)S(1)} %dynamic-slice_bitcast_fusion.2, bf16[1,4,64,32,32]{2,4,3,1,0:T(8,128)(2,1)S(1)} %constant_dynamic-slice_fusion.2), kind=kOutput, calls=%fused_computation.8.clone.1 | convolution fusion | flops 207618048 | bytes 26489344 | tf_op jit(solution)/shard_map/while/body/eval_jaxpr/atpml,apkl->atmk/dot_general | solution.py:25
  480.6 1.3 constant_dynamic-slice_fusion.2
  482.3 10.1 %fusion.44 = f32[4,12,32,64,32]{3,2,4,1,0:T(8,128)} fusion(bf16[4,64,32,32,1]{1,2,3,0,4:T(8,128)(2,1)S(1)} %bitcast.72, bf16[8,4,12,32,32]{4,3,2,1,0:T(8,128)(2,1)S(1)} %get-tuple-element.102, s32[]{:T(128)} %get-tuple-element.94), kind=kOutput, calls=%fused_computation.10.clone.1 | convolution fusion | flops 201326592 | bytes 14024708 | tf_op jit(solution)/shard_map/while/body/eval_jaxpr/apmn,atnl->atpml/dot_general | solution.py:23
  492.4 18.9 %fusion.45 = bf16[8,4,12,32,32]{4,3,2,1,0:T(8,128)(2,1)} fusion(bf16[8,4,12,32,32]{4,3,2,1,0:T(8,128)(2,1)} %get-tuple-element.95, s32[]{:T(128)} %get-tuple-element.94, f32[4,12,32,64,32]{3,2,4,1,0:T(8,128)} %fusion.44, f32[4,12,64]{2,1,0:T(8,128)S(1)} %dynamic-slice_bitcast_fusion.2, bf16[1,4,64,32,32]{2,4,3,1,0:T(8,128)(2,1)S(1)} %constant_dynamic-slice_fusion.2), kind=kOutput, calls=%fused_computation.8.clone.1 | convolution fusion | flops 207618048 | bytes 26489344 | tf_op jit(solution)/shard_map/while/body/eval_jaxpr/atpml,apkl->atmk/dot_general | solution.py:25
  511.3 1.3 constant_dynamic-slice_fusion.2
  513.1 10.1 %fusion.44 = f32[4,12,32,64,32]{3,2,4,1,0:T(8,128)} fusion(bf16[4,64,32,32,1]{1,2,3,0,4:T(8,128)(2,1)S(1)} %bitcast.72, bf16[8,4,12,32,32]{4,3,2,1,0:T(8,128)(2,1)S(1)} %get-tuple-element.102, s32[]{:T(128)} %get-tuple-element.94), kind=kOutput, calls=%fused_computation.10.clone.1 | convolution fusion | flops 201326592 | bytes 14024708 | tf_op jit(solution)/shard_map/while/body/eval_jaxpr/apmn,atnl->atpml/dot_general | solution.py:23
  523.1 18.9 %fusion.45 = bf16[8,4,12,32,32]{4,3,2,1,0:T(8,128)(2,1)} fusion(bf16[8,4,12,32,32]{4,3,2,1,0:T(8,128)(2,1)} %get-tuple-element.95, s32[]{:T(128)} %get-tuple-element.94, f32[4,12,32,64,32]{3,2,4,1,0:T(8,128)} %fusion.44, f32[4,12,64]{2,1,0:T(8,128)S(1)} %dynamic-slice_bitcast_fusion.2, bf16[1,4,64,32,32]{2,4,3,1,0:T(8,128)(2,1)S(1)} %constant_dynamic-slice_fusion.2), kind=kOutput, calls=%fused_computation.8.clone.1 | convolution fusion | flops 207618048 | bytes 26489344 | tf_op jit(solution)/shard_map/while/body/eval_jaxpr/atpml,apkl->atmk/dot_general | solution.py:25
  542.1 5.6 convert_element_type.51
  547.6 22.3 %reduce-scatter.5.cloned.1.call-done = bf16[384,256]{1,0:T(8,128)(2,1)} async-done(((bf16[384,1024]{1,0:T(8,128)(2,1)}), bf16[384,256]{1,0:T(8,128)(2,1)}) %reduce-scatter.5.cloned.1.call-update) | async-done | bytes 196624 | tf_op jit(solution)/shard_map/reduce_scatter | solution.py:65
  (48 shorter events, 3.6 us)
Async XLA Ops:
  6.5 65.0 %reduce-scatter.3.cloned.1.call-start = ((), (), s32[]{:S(2)}) async-start(), calls=%async_computation.3 | async-start | bytes 3932160 | tf_op jit(solution)/shard_map/reduce_scatter | solution.py:46
  26.4 45.1 %copy-start.3 = (s32[1,64,32]{1,2,0:T(8,128)S(1)}, s32[1,64,32]{1,2,0:T(8,128)}, u32[]{:S(2)}) copy-start(s32[1,64,32]{1,2,0:T(8,128)} %param.15) | copy-start | bytes 24580
  28.8 95.6 %all-reduce.2.cloned.1.call-start = ((), (), s32[]{:S(2)}) async-start(), calls=%async_computation.4 | async-start | bytes 1572864 | tf_op jit(solution)/shard_map/psum | solution.py:47
  140.5 11.1 %copy-start.1 = (s32[384,16]{0,1:T(8,128)S(1)}, s32[384,16]{0,1:T(8,128)}, u32[]{:S(2)}) copy-start(s32[384,16]{0,1:T(8,128)} %param.16) | copy-start | bytes 73732
  140.5 105.7 %all-to-all-start = ((bf16[64,32,1024]{2,1,0:T(8,128)(2,1)}), bf16[64,32,1024]{2,1,0:T(8,128)(2,1)}, u32[]{:S(2)}, u32[]{:S(2)}) async-start(bf16[64,32,1024]{2,1,0:T(8,128)(2,1)} %select_select_fusion), calls=%async_computation.1 | async-start | bytes 8388608 | tf_op jit(solution)/shard_map/all_to_all | solution.py:18
  151.4 418.5 %reduce-scatter.5.cloned.1.call-start = ((), (), s32[]{:S(2)}) async-start(), calls=%async_computation.5 | async-start | bytes 983040 | tf_op jit(solution)/shard_map/reduce_scatter | solution.py:65
  152.1 8.6 %copy-start.2 = (f32[384,64]{0,1:T(8,128)S(1)}, f32[384,64]{0,1:T(8,128)}, u32[]{:S(2)}) copy-start(f32[384,64]{0,1:T(8,128)} %param.14) | copy-start | bytes 294916
  152.1 8.7 %copy-start.4 = (s32[384]{0:T(512)S(1)}, s32[384]{0:T(512)}, u32[]{:S(2)}) copy-start(s32[384]{0:T(512)} %param.17) | copy-start | bytes 4612
  152.2 94.1 %copy-start = (bf16[384,1024]{1,0:T(8,128)(2,1)S(1)}, bf16[384,1024]{1,0:T(8,128)(2,1)}, u32[]{:S(2)}) copy-start(bf16[384,1024]{1,0:T(8,128)(2,1)} %all-reduce.2.cloned.1.call-done) | copy-start | bytes 2359300
Sparse Core Ops, SparseCore 0:
  29.0 42.4 reduce-scatter.2
  73.9 50.4 all-reduce.1
  547.8 22.1 reduce-scatter.4
where the time goes:
time: 577 us; the launch traced here: 576 us
  matrix products  238 us (41%)
  waiting for transfers between devices  203 us (35%)
  local copies, waits for them, and re-layouts  84.2 us (15%)
  other arithmetic  26.7 us (5%)
  between operations  13.3 us (2%)
  starting transfers between devices  11.1 us (2%)
    dot_general x8, matrix products, atom_group(): jnp.einsum('atpml,apkl->atmk', inner, coeff, preferred_element_type=jnp.f...  151 us
    all_to_all x1, waiting for transfers between devices, move_blocks(): lax.all_to_all(blocks, ('ka', 'pair'), split_axis=0, concat_axis=0, tiled...  85.3 us
    dot_general x8, matrix products, atom_group(): jnp.einsum('apmn,atnl->atpml', coeff, ymat, preferred_element_type=jnp.fl...  80.7 us
    psum x1, waiting for transfers between devices, shards(): slab = lax.psum(partial_sum, 'aux')  52.5 us
    reduce_scatter x1, waiting for transfers between devices, shards(): lax.psum_scatter(term.astype(jnp.bfloat16), 'ka', scatter_dimension=0, ti...  42.6 us
    gather x1, local copies, waits for them, and re-layouts, shards(): picked = jnp.take(pool, source_index, axis=0)  33.9 us
    reduce_scatter x1, waiting for transfers between devices, shards(): lax.psum_scatter(partial_blocks.astype(jnp.bfloat16), 'aux', scatter_dime...  22.3 us
    dynamic_slice x16, local copies, waits for them, and re-layouts, shards(): lax.map(atom_group, (coeff, ymat, weights)).reshape(target_rows, width)  13.7 us
  transfers between devices with their start and end apart: 4, of which 4 were waited for; matrix products, arithmetic and copies ran while one was open for 2% of the time, Pallas kernels for 0%

commit v1 on v0

v1 whole, which is shorter than its diff:
```python
import math

import jax
import jax.numpy as jnp
from jax import lax
from jax.experimental import pallas as pl
from jax.experimental.pallas import tpu as pltpu
from jax.sharding import PartitionSpec as P

NB = 32
NK = 16
WIDE = 256
ROWS = 128
GROUP = 4
F32 = jnp.float32
BF16 = jnp.bfloat16
NT = (((1,), (1,)), ((), ()))
TN = (((0,), (0,)), ((), ()))


def iota(shape, dim):
    return lax.broadcasted_iota(jnp.int32, shape, dim)


def term_kernel(kp_ref, shift_ref, x_ref, o_ref):
    turns = (
        kp_ref[0, 0] * (NK // 4) * shift_ref[0, 0]
        + kp_ref[0, 1] * (NK // 2) * shift_ref[1, 0]
        + kp_ref[0, 2] * (NK // 2) * shift_ref[2, 0]
    ) & (NK - 1)
    angle = turns.astype(F32) * (2.0 * math.pi / NK)
    row, col = iota((2 * ROWS, ROWS), 0), iota((2 * ROWS, ROWS), 1)
    phase = jnp.where(
        row == 2 * col, jnp.cos(angle) / NK, jnp.where(row == 2 * col + 1, jnp.sin(angle) / NK, 0.0)
    )
    high = phase.astype(BF16)
    low = (phase - high.astype(F32)).astype(BF16)
    block = x_ref[...].reshape(2 * ROWS, x_ref.shape[-1])
    term = lax.dot_general(high, block, TN, preferred_element_type=F32)
    term += lax.dot_general(low, block, TN, preferred_element_type=F32)
    term = term.astype(BF16)
    for j in range(o_ref.shape[1]):
        o_ref[0, j] = term[:, WIDE * j : WIDE * (j + 1)]


def kpoint_terms(kpoint, shift, block):
    slabs, rows = block.shape[:2]
    width = block.shape[-1]
    steps = rows // ROWS
    return pl.pallas_call(
        term_kernel,
        grid=(slabs, steps),
        in_specs=[
            pl.BlockSpec(memory_space=pltpu.SMEM),
            pl.BlockSpec((3, 1, 1, ROWS), lambda g, i: (0, g, 0, i)),
            pl.BlockSpec((ROWS, 2, width), lambda g, i: (g * steps + i, 0, 0)),
        ],
        out_specs=pl.BlockSpec((1, width // WIDE, ROWS, WIDE), lambda g, i: (g, 0, i, 0)),
        out_shape=jax.ShapeDtypeStruct((slabs, width // WIDE, rows, WIDE), BF16),
    )(kpoint, shift.reshape(3, slabs, 1, rows), block.reshape(slabs * rows, 2, width))


def count_kernel(src_ref, len_ref, s_ref):
    rows, pool = s_ref.shape
    lane = iota((rows, pool), 1)
    total = jnp.zeros((rows, pool), F32)
    for g in range(src_ref.shape[1]):
        index = jnp.where(g < len_ref[...], src_ref[:, g : g + 1], -1)
        total += jnp.where(lane == index, 1.0, 0.0)
    s_ref[...] = total.astype(BF16)


def entry_counts(source_index, list_length, pool):
    targets, entries = source_index.shape
    step = 64
    return pl.pallas_call(
        count_kernel,
        grid=(targets // step,),
        in_specs=[
            pl.BlockSpec((step, entries), lambda i: (i, 0)),
            pl.BlockSpec((step, 1), lambda i: (i, 0)),
        ],
        out_specs=pl.BlockSpec((step, pool), lambda i: (i, 0)),
        out_shape=jax.ShapeDtypeStruct((targets, pool), BF16),
    )(source_index, list_length[:, None])


def pick_kernel(terms_ref, rows_ref, slab_ref, sent_ref):
    total = terms_ref[0].astype(F32)
    for k in range(1, terms_ref.shape[0]):
        total += terms_ref[k].astype(F32)
    slab = total.astype(BF16)
    slab_ref[...] = slab
    step = 256
    for i in range(sent_ref.shape[0] // step):
        rows = rows_ref[i * step : (i + 1) * step]
        hot = (rows == iota((step, slab.shape[0]), 1)).astype(F32).astype(BF16)
        sent_ref[i * step : (i + 1) * step] = jnp.dot(
            hot, slab, preferred_element_type=F32
        ).astype(BF16)


def pick(terms, rows):
    return pl.pallas_call(
        pick_kernel,
        out_shape=(
            jax.ShapeDtypeStruct(terms.shape[1:], BF16),
            jax.ShapeDtypeStruct((rows.shape[0], terms.shape[2]), BF16),
        ),
        compiler_params=pltpu.CompilerParams(vmem_limit_bytes=40 * 2**20),
    )(terms, rows)


def list_kernel(counts_ref, slab_ref, got_ref, y_ref):
    own = slab_ref.shape[0]
    total = jnp.dot(counts_ref[:, :own], slab_ref[...], preferred_element_type=F32)
    total += jnp.dot(counts_ref[:, own:], got_ref[...], preferred_element_type=F32)
    y_ref[...] = total.astype(BF16)


def list_sums(counts, slab, got):
    return pl.pallas_call(
        list_kernel,
        out_shape=jax.ShapeDtypeStruct((counts.shape[0], slab.shape[1]), BF16),
        compiler_params=pltpu.CompilerParams(vmem_limit_bytes=40 * 2**20),
    )(counts, slab, got)


def exchange_kernel(pairs_atom, c_ref, y_ref, w_ref, o_ref, y_rows, weighted, folded, gather, diag):
    atoms = c_ref.shape[0]
    targets = atoms * pairs_atom
    quarters = y_ref.shape[0]

    @pl.when(pl.program_id(0) == 0)
    def _():
        shape = (quarters * targets, targets * NB)
        row, col = iota(shape, 0), iota(shape, 1)
        keep = (row % targets == col // NB) & (row // targets == (col % NB) // 8)
        gather[...] = keep.astype(F32).astype(BF16)
        square = (WIDE, WIDE)
        diag[...] = (iota(square, 0) // NB == iota(square, 1) // NB).astype(F32).astype(BF16)

    square = (WIDE, WIDE)
    fold = (iota(square, 0) % NB == iota(square, 1) % NB).astype(F32).astype(BF16)
    spread = (targets, 8, WIDE)
    keep = iota(spread, 2) // NB == iota(spread, 1)
    parts = []
    for j in range(quarters):
        y = y_ref[j].astype(F32)
        parts.append(jnp.where(keep, jnp.broadcast_to(y[:, None, :], spread), 0.0))
    rows = jnp.concatenate(parts, axis=1).reshape(targets * NB, WIDE).astype(BF16)
    y_rows[...] = jnp.dot(rows, fold, preferred_element_type=F32).astype(BF16)
    tall = (pairs_atom * NB, WIDE)
    keep_out = iota(tall, 0) % 8 == iota(tall, 1) // NB

    def atom(a, carry):
        c = c_ref[a]
        for t in range(pairs_atom):
            target = a * pairs_atom + t
            y = y_rows[pl.ds(pl.multiple_of(target * NB, NB), NB), :]
            y = jnp.concatenate([y] * 8, axis=0) * diag[...]
            inner = jnp.dot(c, y, preferred_element_type=F32)
            inner = inner.reshape(8, NB, WIDE) * w_ref[target][:, None, :]
            inner = inner.astype(BF16)
            for p in range(8):
                weighted[p, t * NB : (t + 1) * NB, :] = inner[p]
        total = jnp.zeros(tall, F32)
        for p in range(8):
            copies = jnp.concatenate([c[NB * p : NB * (p + 1), :]] * 8, axis=0)
            total += lax.dot_general(weighted[p], copies, NT, preferred_element_type=F32)
        start = pl.multiple_of(a * pairs_atom * NB, 128)
        folded[pl.ds(start, pairs_atom * NB), :] = jnp.where(keep_out, total, 0.0).astype(BF16)
        return carry

    lax.fori_loop(0, atoms, atom, 0)
    result = jnp.dot(gather[...], folded[...], preferred_element_type=F32).astype(BF16)
    for j in range(quarters):
        o_ref[j] = result[j * targets : (j + 1) * targets]


def exchange(coeff, y, weights):
    atoms = coeff.shape[0]
    quarters, targets = y.shape[:2]
    pairs_atom = targets // atoms
    step = GROUP * pairs_atom

    def kernel(*refs):
        exchange_kernel(pairs_atom, *refs)

    return pl.pallas_call(
        kernel,
        grid=(atoms // GROUP,),
        in_specs=[
            pl.BlockSpec((GROUP, WIDE, WIDE), lambda i: (i, 0, 0)),
            pl.BlockSpec((quarters, step, WIDE), lambda i: (0, i, 0)),
            pl.BlockSpec((step, 8, WIDE), lambda i: (i, 0, 0)),
        ],
        out_specs=pl.BlockSpec((quarters, step, WIDE), lambda i: (0, i, 0)),
        out_shape=jax.ShapeDtypeStruct((quarters, targets, WIDE), BF16),
        scratch_shapes=[
            pltpu.VMEM((step * NB, WIDE), BF16),
            pltpu.VMEM((8, pairs_atom * NB, WIDE), BF16),
            pltpu.VMEM((step * NB, WIDE), BF16),
            pltpu.VMEM((quarters * step, step * NB), BF16),
            pltpu.VMEM((WIDE, WIDE), BF16),
        ],
        compiler_params=pltpu.CompilerParams(vmem_limit_bytes=40 * 2**20),
    )(coeff, y, weights)


def shards(
    kpoint_grid, image_shift, density_k, coefficients, coulomb, send_rows, source_index, list_length
):
    atoms, aux_local = coefficients.shape[:2]
    targets = coulomb.shape[0]
    coeff = coefficients.reshape(atoms, 8, 8, NB, NB)
    coeff = coeff.transpose(0, 1, 3, 2, 4).reshape(atoms, WIDE, WIDE)
    weights = jnp.repeat(coulomb, NB, axis=1).reshape(targets, 8, WIDE)
    slots = send_rows.shape[1] * send_rows.shape[2]
    counts = entry_counts(source_index, list_length, targets + slots)
    rows_out = send_rows.reshape(slots, 1)

    terms = kpoint_terms(kpoint_grid, image_shift, density_k[0])
    terms = terms.reshape(NK, targets, WIDE)
    terms = lax.all_to_all(terms, ("ka", "aux"), split_axis=0, concat_axis=0, tiled=True)
    slab, sent = pick(terms, rows_out)
    sent = sent.reshape(send_rows.shape[1], send_rows.shape[2], WIDE)
    got = lax.all_to_all(sent, ("ka", "pair"), split_axis=0, concat_axis=0, tiled=True)
    y = list_sums(counts, slab, got.reshape(slots, WIDE))
    y = lax.all_gather(y, "aux")
    partial = exchange(coeff, y, weights)
    parts = lax.all_to_all(partial, "aux", split_axis=0, concat_axis=0, tiled=True)
    return jnp.sum(parts.astype(F32), axis=0).astype(BF16)


def solution(mesh):
    placed = (
        P(("ka", "aux"), None),
        P(None, None, "pair"),
        P(("ka", "aux"), None, "pair", None, None),
        P(("ka", "pair"), "aux", None),
        P(("ka", "pair"), "aux"),
        P(("ka", "pair"), None, None),
        P(("ka", "pair"), None),
        P(("ka", "pair")),
    )
    return jax.shard_map(
        shards, mesh=mesh, in_specs=placed, out_specs=P(("ka", "pair"), "aux"), check_vma=False
    )
```

time: 577 us -> 227 us (0.39)
  matrix products: 238 us -> 0 us
  waiting for transfers between devices: 203 us -> 38.9 us
  Pallas kernels: 0 us -> 64.1 us
  blocking collectives: 0 us -> 29.7 us
  other arithmetic: 26.7 us -> 0.82 us
  between operations: 13.3 us -> 0.07 us
  local copies, waits for them, and re-layouts: 84.2 us -> 71.5 us
  starting transfers between devices: 11.1 us -> 20 us
    dot_general x17 -> x0, matrix products: 238 us -> none  [the longest x8 151 us: atom_group(): jnp.einsum('atpml,apkl->atmk', inner, coeff, preferred_element_type=jnp.f...]
    reduce_scatter x2 -> x0, waiting for transfers between devices: 64.9 us -> none  [the longest x1 42.6 us: shards(): lax.psum_scatter(term.astype(jnp.bfloat16), 'ka', scatter_dimension=0, ti...]
    pallas_call x0 -> x5, Pallas kernels: none -> 64.1 us  [the longest x1 38 us: exchange(): pl.pallas_call(kernel, grid=(atoms // GROUP,), in_specs=[pl.BlockSpec((GR...]
    reshape x2 -> x5, local copies, waits for them, and re-layouts: 3.78 us -> 61.4 us  [the longest x2 37.6 us: shards(): coeff = coefficients.reshape(atoms, 8, 8, NB, NB)]
    psum x1 -> x0, waiting for transfers between devices: 52.5 us -> none  [shards(): slab = lax.psum(partial_sum, 'aux')]
    all_to_all x1 -> x2, waiting for transfers between devices: 85.3 us -> 38.9 us  [the longest x1 38.9 us: shards(): lax.all_to_all(terms, ('ka', 'aux'), split_axis=0, concat_axis=0, tiled=T...]
    gather x2 -> x0, local copies, waits for them, and re-layouts: 46.1 us -> none  [the longest x1 33.9 us: shards(): picked = jnp.take(pool, source_index, axis=0)]
    all_gather x0 -> x1, blocking collectives: none -> 15.6 us  [shards(): y = lax.all_gather(y, 'aux')]
  transfers between devices with their start and end apart: 4 -> 2, of which waited for: 4 -> 1; matrix products, arithmetic and copies ran while one was open for 2% -> 29% of each run, Pallas kernels for 0% -> 5%
where the time goes in v1:
time: 227 us; the launch traced here: 225 us
  local copies, waits for them, and re-layouts  71.5 us (31%)
  Pallas kernels  64.1 us (28%)
  waiting for transfers between devices  38.9 us (17%)
  blocking collectives  29.7 us (13%)
  starting transfers between devices  20 us (9%)
    all_to_all x1, waiting for transfers between devices, shards(): lax.all_to_all(terms, ('ka', 'aux'), split_axis=0, concat_axis=0, tiled=T...  38.9 us
    pallas_call x1, Pallas kernels, exchange(): pl.pallas_call(kernel, grid=(atoms // GROUP,), in_specs=[pl.BlockSpec((GR...  38 us
    reshape x2, local copies, waits for them, and re-layouts, shards(): coeff = coefficients.reshape(atoms, 8, 8, NB, NB)  37.6 us
    reshape x1, local copies, waits for them, and re-layouts, shards(): coeff = coeff.transpose(0, 1, 3, 2, 4).reshape(atoms, WIDE, WIDE)  20.4 us
    all_gather x1, blocking collectives, shards(): y = lax.all_gather(y, 'aux')  15.6 us
    all_to_all x1, blocking collectives, shards(): lax.all_to_all(partial, 'aux', split_axis=0, concat_axis=0, tiled=True)  14.1 us
    all_to_all x1, starting transfers between devices, shards(): lax.all_to_all(sent, ('ka', 'pair'), split_axis=0, concat_axis=0, tiled=T...  12.4 us
    pallas_call x1, Pallas kernels, entry_counts(): pl.pallas_call(count_kernel, grid=(targets // step,), in_specs=[pl.BlockS...  12 us
  transfers between devices with their start and end apart: 2, of which 1 were waited for; matrix products, arithmetic and copies ran while one was open for 29% of the time, Pallas kernels for 5%

profile of v1, /device:TPU:2, one launch (start us, length us, event | category | flops | bytes accessed | tf_op | source)
XLA Modules:
  0.0 225.1 jit_solution(17726860183646854450)
XLA Ops:
  0.0 1.3 reshape.23.shift_ref
  1.3 10.9 %shard_map.83 = bf16[4,4,384,256]{3,2,1,0:T(8,128)(2,1)} custom-call(s32[1,3]{1,0:T(1,128)} %kp_ref.1, s32[3,4,1,384]{3,2,1,0:T(1,128)} %reshape.23.shift_ref, bf16[1536,2,1024]{2,1,0:T(2,128)(2,1)} %bitcast.16), custom_call_target="tpu_custom_call" | custom-call | tf_op jit(solution)/shard_map/pallas_call | solution.py:50
  12.3 0.0 copy-start.6
  12.3 7.6 %all-to-all-start = ((bf16[16,384,256]{2,1,0:T(8,128)(2,1)}), bf16[16,384,256]{2,1,0:T(8,128)(2,1)S(1)}, u32[]{:S(2)}, u32[]{:S(2)}) async-start(bf16[16,384,256]{2,1,0:T(8,128)(2,1)} %bitcast.15), calls=%async_computation | async-start | bytes 6291456 | tf_op jit(solution)/shard_map/all_to_all | solution.py:225
  19.9 0.0 copy-done.6
  19.9 0.1 copy.16
  20.0 2.1 reshape.29.rows_ref
  22.1 38.9 %all-to-all-done.terms_ref = bf16[16,384,256]{2,1,0:T(8,128)(2,1)S(1)} async-done(((bf16[16,384,256]{2,1,0:T(8,128)(2,1)}), bf16[16,384,256]{2,1,0:T(8,128)(2,1)S(1)}, u32[]{:S(2)}, u32[]{:S(2)}) %all-to-all-start) | async-done | bytes 3145760 | tf_op jit(solution)/shard_map/all_to_all | solution.py:225
  61.0 0.0 copy-start.2
  61.0 1.2 copy-done.2
  62.2 1.0 shard_map.84
  63.2 0.0 copy-start.3
  63.3 1.0 copy-done.3
  64.3 12.4 %all-to-all-start.1 = ((bf16[64,32,256]{2,1,0:T(8,128)(2,1)}), bf16[64,32,256]{2,1,0:T(8,128)(2,1)}, u32[]{:S(2)}, u32[]{:S(2)}) async-start(bf16[64,32,256]{2,1,0:T(8,128)(2,1)} %bitcast.12), calls=%async_computation.1 | async-start | bytes 2097152 | tf_op jit(solution)/shard_map/all_to_all | solution.py:228
  76.7 20.3 %reshape.21 = bf16[32,8,8,32,32]{4,3,2,1,0:T(8,128)(2,1)} reshape(bf16[32,64,1024]{2,1,0:T(8,128)(2,1)} %param.11) | data formatting | bytes 8388608 | tf_op jit(solution)/shard_map/reshape | solution.py:216
  97.0 17.3 %copy.20 = bf16[32,8,8,32,32]{4,2,3,1,0:T(8,128)(2,1)} copy(bf16[32,8,8,32,32]{4,3,2,1,0:T(8,128)(2,1)} %reshape.21) | data formatting | bytes 8388608 | tf_op jit(solution)/shard_map/reshape | solution.py:216
  114.3 0.0 copy-start.5
  114.3 0.0 copy-start.7
  114.3 0.0 copy-start.4
  114.3 20.4 %reshape.22.refs_0_ = bf16[32,256,256]{2,1,0:T(8,128)(2,1)} reshape(bf16[32,8,32,8,32]{4,3,2,1,0:T(8,128)(2,1)} %bitcast.13) | data formatting | bytes 8388608 | tf_op jit(solution)/shard_map/reshape | solution.py:217
  134.7 0.0 copy-done.5
  134.7 0.8 copy.14.src_ref
  135.5 0.0 copy-done.7
  135.5 0.8 broadcast_in_dim.8.len_ref
  136.3 0.0 copy-done.4
  136.3 1.8 broadcast_in_dim.7
  138.1 2.7 %copy.18.refs_2_ = f32[384,8,256]{2,1,0:T(8,128)S(1)} copy(f32[384,8,256]{0,2,1:T(8,128)} %bitcast.14) | data formatting | bytes 6291456 | tf_op jit(solution)/shard_map/reshape;reshape | solution.py:218
  140.8 12.0 %shard_map.82.counts_ref = bf16[384,2432]{1,0:T(8,128)(2,1)} custom-call(s32[384,16]{1,0:T(8,128)} %copy.14.src_ref, s32[384,1]{1,0:T(8,128)} %broadcast_in_dim.8.len_ref), custom_call_target="tpu_custom_call" | custom-call | tf_op jit(solution)/shard_map/pallas_call | solution.py:76
  152.8 0.0 all-to-all-done.1
  152.8 0.0 copy-start
  152.8 0.0 copy-start.1
  152.8 1.7 copy-done.1
  154.5 2.1 shard_map.85
  156.5 15.6 %all-gather = bf16[1536,256]{1,0:T(8,128)(2,1)S(1)} all-gather(bf16[384,256]{1,0:T(8,128)(2,1)S(1)} %shard_map.85), channel_id=2, replica_groups=mesh['ka'=4,'pair'=16,'aux'=4] {'aux'}, dimensions={0}, use_global_device_ids=true | all-gather | bytes 983040 | tf_op jit(solution)/shard_map/all_gather | solution.py:230
  172.1 0.0 copy-done
  172.1 38.0 %shard_map.86 = bf16[4,384,256]{2,1,0:T(8,128)(2,1)S(1)} custom-call(bf16[32,256,256]{2,1,0:T(8,128)(2,1)S(1)} %copy-done, bf16[4,384,256]{2,1,0:T(8,128)(2,1)S(1)} %bitcast.11, f32[384,8,256]{2,1,0:T(8,128)S(1)} %copy.18.refs_2_), custom_call_target="tpu_custom_call" | custom-call | tf_op jit(solution)/shard_map/pallas_call | solution.py:190
  210.1 14.1 %all_to_all.15 = bf16[4,384,256]{2,1,0:T(8,128)(2,1)S(1)} all-to-all(bf16[4,384,256]{2,1,0:T(8,128)(2,1)S(1)} %shard_map.86), channel_id=1, replica_groups=mesh['ka'=4,'pair'=16,'aux'=4] {'aux'}, dimensions={0} | all-to-all | bytes 1572864 | tf_op jit(solution)/shard_map/all_to_all | solution.py:232
  224.3 0.8 reduce_sum.12
Async XLA Ops:
  12.3 7.6 %copy-start.6 = (s32[1,64,32]{1,2,0:T(8,128)S(1)}, s32[1,64,32]{1,2,0:T(8,128)}, u32[]{:S(2)}) copy-start(s32[1,64,32]{1,2,0:T(8,128)} %param.13) | copy-start | bytes 24580
  12.3 48.7 %all-to-all-start = ((bf16[16,384,256]{2,1,0:T(8,128)(2,1)}), bf16[16,384,256]{2,1,0:T(8,128)(2,1)S(1)}, u32[]{:S(2)}, u32[]{:S(2)}) async-start(bf16[16,384,256]{2,1,0:T(8,128)(2,1)} %bitcast.15), calls=%async_computation | async-start | bytes 6291456 | tf_op jit(solution)/shard_map/all_to_all | solution.py:225
  61.0 1.2 copy-start.2
  63.2 1.0 copy-start.3
  64.3 88.5 %all-to-all-start.1 = ((bf16[64,32,256]{2,1,0:T(8,128)(2,1)}), bf16[64,32,256]{2,1,0:T(8,128)(2,1)}, u32[]{:S(2)}, u32[]{:S(2)}) async-start(bf16[64,32,256]{2,1,0:T(8,128)(2,1)} %bitcast.12), calls=%async_computation.1 | async-start | bytes 2097152 | tf_op jit(solution)/shard_map/all_to_all | solution.py:228
  114.3 20.4 %copy-start.5 = (s32[384,16]{0,1:T(8,128)S(1)}, s32[384,16]{0,1:T(8,128)}, u32[]{:S(2)}) copy-start(s32[384,16]{0,1:T(8,128)} %param.14) | copy-start | bytes 73732
  114.3 21.2 %copy-start.7 = (s32[384]{0:T(512)S(1)}, s32[384]{0:T(512)}, u32[]{:S(2)}) copy-start(s32[384]{0:T(512)} %param.15) | copy-start | bytes 4612
  114.3 22.0 %copy-start.4 = (f32[384,64]{0,1:T(8,128)S(1)}, f32[384,64]{0,1:T(8,128)}, u32[]{:S(2)}) copy-start(f32[384,64]{0,1:T(8,128)} %param.12) | copy-start | bytes 294916
  152.8 19.3 %copy-start = (bf16[32,256,256]{2,1,0:T(8,128)(2,1)S(1)}, bf16[32,256,256]{2,1,0:T(8,128)(2,1)}, u32[]{:S(2)}) copy-start(bf16[32,256,256]{2,1,0:T(8,128)(2,1)} %reshape.22.refs_0_) | copy-start | bytes 12582916
  152.8 1.7 copy-start.1

commit v2 on v1

v2 whole, which is shorter than its diff:
```python
import math

import jax
import jax.numpy as jnp
from jax import lax
from jax.experimental import pallas as pl
from jax.experimental.pallas import tpu as pltpu
from jax.sharding import PartitionSpec as P

NB = 32
NK = 16
WIDE = 256
ROWS = 128
GROUP = 4
QUARTERS = 4
AXES = ("ka", "pair", "aux")
F32 = jnp.float32
BF16 = jnp.bfloat16
NT = (((1,), (1,)), ((), ()))
TN = (((0,), (0,)), ((), ()))


def iota(shape, dim):
    return lax.broadcasted_iota(jnp.int32, shape, dim)


def term_kernel(kp_ref, me_ref, shift_ref, x_ref, o_ref):
    g = pl.program_id(0)
    rows, _, width = x_ref.shape
    turns = (
        kp_ref[0, 0] * (NK // 4) * shift_ref[0, 0]
        + kp_ref[0, 1] * (NK // 2) * shift_ref[1, 0]
        + kp_ref[0, 2] * (NK // 2) * shift_ref[2, 0]
    ) & (NK - 1)
    angle = turns.astype(F32) * (2.0 * math.pi / NK)
    even, odd = jnp.cos(angle) / NK, jnp.sin(angle) / NK
    row, col = iota((2 * ROWS, ROWS), 0), iota((2 * ROWS, ROWS), 1)
    core, second = me_ref[0], me_ref[1]
    for i in range(rows // ROWS):
        here = slice(i * ROWS, (i + 1) * ROWS)
        phase = jnp.where(
            row == 2 * col, even[:, here], jnp.where(row == 2 * col + 1, odd[:, here], 0.0)
        )
        high = phase.astype(BF16)
        low = (phase - high.astype(F32)).astype(BF16)
        both = jnp.concatenate([high, low], axis=1).T
        block = x_ref[here].reshape(2 * ROWS, width)
        term = jnp.dot(both, block, preferred_element_type=F32)
        term = (term[:ROWS] + term[ROWS:]).astype(BF16)
        for j in range(width // WIDE):
            first = jnp.where(core == 0, g, j)
            other = (jnp.where(core == 0, j, g) - second) & 3
            o_ref[first, other, here] = term[:, WIDE * j : WIDE * (j + 1)]


def kpoint_terms(kpoint, me, shift, block):
    slabs, rows = block.shape[:2]
    width = block.shape[-1]
    shape = (slabs, width // WIDE, rows, WIDE)
    return pl.pallas_call(
        term_kernel,
        grid=(slabs,),
        in_specs=[
            pl.BlockSpec(memory_space=pltpu.SMEM),
            pl.BlockSpec(memory_space=pltpu.SMEM),
            pl.BlockSpec((3, 1, 1, rows), lambda g: (0, g, 0, 0)),
            pl.BlockSpec((rows, 2, width), lambda g: (g, 0, 0)),
        ],
        out_specs=pl.BlockSpec(shape, lambda g: (0, 0, 0, 0)),
        out_shape=jax.ShapeDtypeStruct(shape, BF16),
        compiler_params=pltpu.CompilerParams(vmem_limit_bytes=40 * 2**20),
    )(kpoint, me, shift.reshape(3, slabs, 1, rows), block.reshape(slabs * rows, 2, width))


def half_sum_kernel(x_ref, *o_refs):
    for q, o_ref in enumerate(o_refs):
        total = x_ref[0, q].astype(F32)
        for f in range(1, x_ref.shape[0]):
            total += x_ref[f, q].astype(F32)
        o_ref[...] = total.astype(BF16)


def half_sums(terms):
    parts, others, rows, width = terms.shape
    step = rows // 3
    return pl.pallas_call(
        half_sum_kernel,
        grid=(rows // step,),
        in_specs=[pl.BlockSpec((parts, others, step, width), lambda i: (0, 0, i, 0))],
        out_specs=[pl.BlockSpec((step, width), lambda i: (i, 0))] * others,
        out_shape=[jax.ShapeDtypeStruct((rows, width), BF16)] * others,
        compiler_params=pltpu.CompilerParams(vmem_limit_bytes=40 * 2**20),
    )(terms)


def relay_kernel(x_ref, o_ref, wide, place):
    @pl.when(pl.program_id(0) == 0)
    def _():
        row, col = iota((WIDE, WIDE), 0), iota((WIDE, WIDE), 1)
        for p in range(8):
            keep = (row % NB == col % NB) & (col // NB == p)
            place[p] = keep.astype(F32).astype(BF16)

    wide[...] = x_ref[0].astype(F32)
    keep = iota((8, WIDE), 0) == iota((8, WIDE), 1) // NB
    total = jnp.zeros((WIDE, WIDE), F32)
    for p in range(8):
        rows = []
        for q in range(8):
            for j in range(4):
                row = wide[8 * q + p : 8 * q + p + 1, WIDE * j : WIDE * (j + 1)]
                rows.append(jnp.where(keep, jnp.broadcast_to(row, (8, WIDE)), 0.0))
        rows = jnp.concatenate(rows, axis=0).astype(BF16)
        total += jnp.dot(rows, place[p], preferred_element_type=F32)
    o_ref[0] = total.astype(BF16)


def relay_coefficients(coefficients):
    atoms, aux, width = coefficients.shape
    return pl.pallas_call(
        relay_kernel,
        grid=(atoms,),
        in_specs=[pl.BlockSpec((1, aux, width), lambda i: (i, 0, 0))],
        out_specs=pl.BlockSpec((1, WIDE, WIDE), lambda i: (i, 0, 0)),
        out_shape=jax.ShapeDtypeStruct((atoms, WIDE, WIDE), BF16),
        scratch_shapes=[pltpu.VMEM((aux, width), F32), pltpu.VMEM((8, WIDE, WIDE), BF16)],
    )(coefficients)


def count_kernel(src_ref, len_ref, coul_ref, s_ref, w_ref):
    coul = coul_ref[...]
    rows, aux = coul.shape
    high = coul.astype(BF16)
    rest = coul - high.astype(F32)
    middle = rest.astype(BF16)
    pieces = [high, middle, (rest - middle.astype(F32)).astype(BF16)]
    for p in range(aux // 8):
        keep = iota((aux, WIDE), 0) == 8 * p + iota((aux, WIDE), 1) // NB
        keep = keep.astype(F32).astype(BF16)
        spread = [jnp.dot(piece, keep, preferred_element_type=F32) for piece in pieces]
        w_ref[:, p, :] = (spread[0] + spread[1]) + spread[2]
    rows, pool = s_ref.shape
    lane = iota((rows, pool), 1)
    total = jnp.zeros((rows, pool), F32)
    for g in range(src_ref.shape[1]):
        index = jnp.where(g < len_ref[...], src_ref[:, g : g + 1], -1)
        total += jnp.where(lane == index, 1.0, 0.0)
    s_ref[...] = total.astype(BF16)


def entry_counts(source_index, list_length, coulomb, pool):
    targets, entries = source_index.shape
    aux = coulomb.shape[1]
    step = 64
    return pl.pallas_call(
        count_kernel,
        grid=(targets // step,),
        in_specs=[
            pl.BlockSpec((step, entries), lambda i: (i, 0)),
            pl.BlockSpec((step, 1), lambda i: (i, 0)),
            pl.BlockSpec((step, aux), lambda i: (i, 0)),
        ],
        out_specs=[
            pl.BlockSpec((step, pool), lambda i: (i, 0)),
            pl.BlockSpec((step, aux // 8, WIDE), lambda i: (i, 0, 0)),
        ],
        out_shape=[
            jax.ShapeDtypeStruct((targets, pool), BF16),
            jax.ShapeDtypeStruct((targets, aux // 8, WIDE), F32),
        ],
    )(source_index, list_length[:, None], coulomb)


def pick_kernel(rows_ref, own_ref, a_ref, b_ref, c_ref, slab_ref, sent_ref):
    total = own_ref[...].astype(F32) + a_ref[...].astype(F32)
    total += b_ref[...].astype(F32) + c_ref[...].astype(F32)
    slab = total.astype(BF16)
    slab_ref[...] = slab
    step = 256
    for i in range(sent_ref.shape[0] // step):
        rows = rows_ref[i * step : (i + 1) * step]
        hot = (rows == iota((step, slab.shape[0]), 1)).astype(F32).astype(BF16)
        sent_ref[i * step : (i + 1) * step] = jnp.dot(
            hot, slab, preferred_element_type=F32
        ).astype(BF16)


def pick(rows, parts):
    shape = parts[0].shape
    return pl.pallas_call(
        pick_kernel,
        out_shape=(
            jax.ShapeDtypeStruct(shape, BF16),
            jax.ShapeDtypeStruct((rows.shape[0], shape[1]), BF16),
        ),
        compiler_params=pltpu.CompilerParams(vmem_limit_bytes=40 * 2**20),
    )(rows, *parts)


def list_kernel(counts_ref, slab_ref, got_ref, y_ref):
    own = slab_ref.shape[0]
    total = jnp.dot(counts_ref[:, :own], slab_ref[...], preferred_element_type=F32)
    total += jnp.dot(counts_ref[:, own:], got_ref[...], preferred_element_type=F32)
    y_ref[...] = total.astype(BF16)


def list_sums(counts, slab, got):
    return pl.pallas_call(
        list_kernel,
        out_shape=jax.ShapeDtypeStruct((counts.shape[0], slab.shape[1]), BF16),
        compiler_params=pltpu.CompilerParams(vmem_limit_bytes=40 * 2**20),
    )(counts, slab, got)


def exchange_kernel(pairs_atom, me_ref, c_ref, w_ref, *refs):
    y_refs, o_refs = refs[:QUARTERS], refs[QUARTERS : 2 * QUARTERS]
    y_all, y_rows, weighted, folded, gather, diag = refs[2 * QUARTERS :]
    atoms = c_ref.shape[0]
    targets = atoms * pairs_atom
    me = me_ref[0]

    @pl.when(pl.program_id(0) == 0)
    def _():
        shape = (QUARTERS * targets, targets * NB)
        row, col = iota(shape, 0), iota(shape, 1)
        quarter = (row // targets + me) & 3
        keep = (row % targets == col // NB) & (quarter == (col % NB) // 8)
        gather[...] = keep.astype(F32).astype(BF16)
        square = (WIDE, WIDE)
        diag[...] = (iota(square, 0) // NB == iota(square, 1) // NB).astype(F32).astype(BF16)

    square = (WIDE, WIDE)
    fold = (iota(square, 0) % NB == iota(square, 1) % NB).astype(F32).astype(BF16)
    spread = (targets, 8, WIDE)
    keep = iota(spread, 2) // NB == iota(spread, 1)
    for r, y_ref in enumerate(y_refs):
        y_all[(me + r) & 3] = y_ref[...].astype(F32)
    parts = []
    for j in range(QUARTERS):
        parts.append(jnp.where(keep, jnp.broadcast_to(y_all[j][:, None, :], spread), 0.0))
    rows = jnp.concatenate(parts, axis=1).reshape(targets * NB, WIDE).astype(BF16)
    y_rows[...] = jnp.dot(rows, fold, preferred_element_type=F32).astype(BF16)
    tall = (pairs_atom * NB, WIDE)
    keep_out = iota(tall, 0) % 8 == iota(tall, 1) // NB

    def atom(a, carry):
        c = c_ref[a]
        for t in range(pairs_atom):
            target = a * pairs_atom + t
            y = y_rows[pl.ds(pl.multiple_of(target * NB, NB), NB), :]
            y = jnp.concatenate([y] * 8, axis=0) * diag[...]
            inner = jnp.dot(c, y, preferred_element_type=F32)
            inner = inner.reshape(8, NB, WIDE) * w_ref[target][:, None, :]
            inner = inner.astype(BF16)
            for p in range(8):
                weighted[p, t * NB : (t + 1) * NB, :] = inner[p]
        total = jnp.zeros(tall, F32)
        for p in range(8):
            copies = jnp.concatenate([c[NB * p : NB * (p + 1), :]] * 8, axis=0)
            total += lax.dot_general(weighted[p], copies, NT, preferred_element_type=F32)
        start = pl.multiple_of(a * pairs_atom * NB, 128)
        folded[pl.ds(start, pairs_atom * NB), :] = jnp.where(keep_out, total, 0.0).astype(BF16)
        return carry

    lax.fori_loop(0, atoms, atom, 0)
    result = jnp.dot(gather[...], folded[...], preferred_element_type=F32).astype(BF16)
    for r, o_ref in enumerate(o_refs):
        o_ref[...] = result[r * targets : (r + 1) * targets]


def exchange(me, coeff, weights, quarters):
    atoms = coeff.shape[0]
    targets = weights.shape[0]
    pairs_atom = targets // atoms
    step = GROUP * pairs_atom
    part = pl.BlockSpec((step, WIDE), lambda i: (i, 0))

    def kernel(*refs):
        exchange_kernel(pairs_atom, *refs)

    return pl.pallas_call(
        kernel,
        grid=(atoms // GROUP,),
        in_specs=[
            pl.BlockSpec(memory_space=pltpu.SMEM),
            pl.BlockSpec((GROUP, WIDE, WIDE), lambda i: (i, 0, 0)),
            pl.BlockSpec((step, 8, WIDE), lambda i: (i, 0, 0)),
        ]
        + [part] * QUARTERS,
        out_specs=[part] * QUARTERS,
        out_shape=[jax.ShapeDtypeStruct((targets, WIDE), BF16)] * QUARTERS,
        scratch_shapes=[
            pltpu.VMEM((QUARTERS, step, WIDE), F32),
            pltpu.VMEM((step * NB, WIDE), BF16),
            pltpu.VMEM((8, pairs_atom * NB, WIDE), BF16),
            pltpu.VMEM((step * NB, WIDE), BF16),
            pltpu.VMEM((QUARTERS * step, step * NB), BF16),
            pltpu.VMEM((WIDE, WIDE), BF16),
        ],
        compiler_params=pltpu.CompilerParams(vmem_limit_bytes=40 * 2**20),
    )(me, coeff, weights, *quarters)


def rank(mesh, k, p, a):
    return (k % mesh.shape["ka"] * mesh.shape["pair"] + p) * mesh.shape["aux"] + a % mesh.shape["aux"]


def first_groups(mesh):
    ka, pair, aux = (mesh.shape[n] for n in AXES)
    groups = []
    for p in range(pair):
        if p % 2 == 0:
            groups += [[rank(mesh, k, p, a) for k in range(ka)] for a in range(aux)]
        else:
            groups += [[rank(mesh, k, p, a) for a in range(aux)] for k in range(ka)]
    return groups


def second_shift(mesh, by):
    ka, pair, aux = (mesh.shape[n] for n in AXES)
    pairs = []
    for k in range(ka):
        for p in range(pair):
            for a in range(aux):
                to = rank(mesh, k, p, a + by) if p % 2 == 0 else rank(mesh, k + by, p, a)
                pairs.append((rank(mesh, k, p, a), to))
    return pairs


def along_aux(array, by):
    return lax.ppermute(array, "aux", [(i, (i + by) % QUARTERS) for i in range(QUARTERS)])


def make_shards(mesh):
    def shards(
        kpoint_grid,
        image_shift,
        density_k,
        coefficients,
        coulomb,
        send_rows,
        source_index,
        list_length,
    ):
        targets = coulomb.shape[0]
        slots = send_rows.shape[1] * send_rows.shape[2]
        core = lax.axis_index("pair") % 2
        aux = lax.axis_index("aux")
        second = jnp.where(core == 0, aux, lax.axis_index("ka"))
        me = jnp.stack([core, second]).astype(jnp.int32)

        terms = kpoint_terms(kpoint_grid, me, image_shift, density_k[0])
        terms, coulomb, source_index, list_length, send_rows = lax.optimization_barrier(
            (terms, coulomb, source_index, list_length, send_rows)
        )
        terms = lax.all_to_all(
            terms, AXES, split_axis=0, concat_axis=0, tiled=True, axis_index_groups=first_groups(mesh)
        )
        counts, weights = entry_counts(source_index, list_length, coulomb, targets + slots)
        rows_out = send_rows.reshape(slots, 1)
        terms, weights, counts, rows_out = lax.optimization_barrier(
            (terms, weights, counts, rows_out)
        )
        halves = half_sums(terms)
        parts = [halves[0]] + [
            lax.ppermute(halves[by], AXES, second_shift(mesh, by)) for by in (2, 1, 3)
        ]
        slab, sent = pick(rows_out, parts)
        sent, coefficients = lax.optimization_barrier((sent, coefficients))
        sent = sent.reshape(send_rows.shape[1], send_rows.shape[2], WIDE)
        got = lax.all_to_all(sent, ("ka", "pair"), split_axis=0, concat_axis=0, tiled=True)
        coeff = relay_coefficients(coefficients)
        got, coeff = lax.optimization_barrier((got, coeff))
        y = list_sums(counts, slab, got.reshape(slots, WIDE))
        far, right, left = along_aux(y, 2), along_aux(y, -1), along_aux(y, 1)
        own, a, b, c = exchange(aux.reshape(1).astype(jnp.int32), coeff, weights, (y, right, far, left))
        total = own.astype(F32) + along_aux(b, 2).astype(F32)
        total += along_aux(a, 1).astype(F32) + along_aux(c, 3).astype(F32)
        return total.astype(BF16)

    return shards


def solution(mesh):
    placed = (
        P(("ka", "aux"), None),
        P(None, None, "pair"),
        P(("ka", "aux"), None, "pair", None, None),
        P(("ka", "pair"), "aux", None),
        P(("ka", "pair"), "aux"),
        P(("ka", "pair"), None, None),
        P(("ka", "pair"), None),
        P(("ka", "pair")),
    )
    return jax.shard_map(
        make_shards(mesh),
        mesh=mesh,
        in_specs=placed,
        out_specs=P(("ka", "pair"), "aux"),
        check_vma=False,
    )
```

time: 227 us -> 158 us (0.70)
  local copies, waits for them, and re-layouts: 71.5 us -> 10.9 us
  blocking collectives: 29.7 us -> 0 us
  Pallas kernels: 64.1 us -> 82.9 us
  starting transfers between devices: 20 us -> 31.5 us
  waiting for transfers between devices: 38.9 us -> 29 us
    reshape x3 -> x0, local copies, waits for them, and re-layouts: 58 us -> none  [the longest x2 37.6 us: shards(): coeff = coefficients.reshape(atoms, 8, 8, NB, NB)]
    all_to_all x1, waiting for transfers between devices: 38.9 us -> 4.87 us  [shards(): lax.all_to_all(terms, AXES, split_axis=0, concat_axis=0, tiled=True, axis...]
    ppermute x0 -> x9, waiting for transfers between devices: none -> 21.4 us  [the longest x6 17.6 us: along_aux(): lax.ppermute(array, 'aux', [(i, (i + by) % QUARTERS) for i in range(QUART...]
    pallas_call x3 -> x5, Pallas kernels: 50 us -> 69 us  [the longest x1 37.9 us: exchange(): pl.pallas_call(kernel, grid=(atoms // GROUP,), in_specs=[pl.BlockSpec(mem...]
    all_gather x1 -> x0, blocking collectives: 15.6 us -> none  [shards(): y = lax.all_gather(y, 'aux')]
    ppermute x0 -> x9, starting transfers between devices: none -> 14.7 us  [the longest x6 9.35 us: along_aux(): lax.ppermute(array, 'aux', [(i, (i + by) % QUARTERS) for i in range(QUART...]
    all_to_all x1 -> x0, blocking collectives: 14.1 us -> none  [shards(): lax.all_to_all(partial, 'aux', split_axis=0, concat_axis=0, tiled=True)]
    all_to_all x1, waiting for transfers between devices: 0.01 us -> 2.75 us  [shards(): lax.all_to_all(sent, ('ka', 'pair'), split_axis=0, concat_axis=0, tiled=T...]
  transfers between devices with their start and end apart: 2 -> 11, of which waited for: 1 -> 8; matrix products, arithmetic and copies ran while one was open for 29% -> 2% of each run, Pallas kernels for 5% -> 24%
where the time goes in v2:
time: 158 us; the launch traced here: 155 us
  Pallas kernels  82.9 us (52%)
  starting transfers between devices  31.5 us (20%)
  waiting for transfers between devices  29 us (18%)
  local copies, waits for them, and re-layouts  10.9 us (7%)
    pallas_call x1, Pallas kernels, exchange(): pl.pallas_call(kernel, grid=(atoms // GROUP,), in_specs=[pl.BlockSpec(mem...  37.9 us
    pallas_call x1, Pallas kernels, relay_coefficients(): pl.pallas_call(relay_kernel, grid=(atoms,), in_specs=[pl.BlockSpec((1, au...  24.4 us
    ppermute x6, waiting for transfers between devices, along_aux(): lax.ppermute(array, 'aux', [(i, (i + by) % QUARTERS) for i in range(QUART...  17.6 us
    pallas_call x1, Pallas kernels, entry_counts(): pl.pallas_call(count_kernel, grid=(targets // step,), in_specs=[pl.BlockS...  13.2 us
    all_to_all x1, starting transfers between devices, shards(): lax.all_to_all(sent, ('ka', 'pair'), split_axis=0, concat_axis=0, tiled=T...  10.8 us
    ppermute x6, starting transfers between devices, along_aux(): lax.ppermute(array, 'aux', [(i, (i + by) % QUARTERS) for i in range(QUART...  9.35 us
    unnamed x20, local copies, waits for them, and re-layouts  7.27 us
    all_to_all x1, starting transfers between devices, shards(): lax.all_to_all(terms, AXES, split_axis=0, concat_axis=0, tiled=True, axis...  6.08 us
  transfers between devices with their start and end apart: 11, of which 8 were waited for; matrix products, arithmetic and copies ran while one was open for 2% of the time, Pallas kernels for 24%

profile of v2, /device:TPU:2, one launch (start us, length us, event | category | flops | bytes accessed | tf_op | source)
XLA Modules:
  0.0 155.3 jit_solution(12192371635679544515)
XLA Ops:
  0.0 0.7 reshape.16.shift_ref
  0.7 0.1 pad_add_fusion.me_ref
  0.8 2.8 %copy-done.2 = bf16[1,4,384,2,1024]{4,3,2,1,0:T(2,128)(2,1)S(1)} copy-done((bf16[1,4,384,2,1024]{4,3,2,1,0:T(2,128)(2,1)S(1)}, bf16[1,4,384,2,1024]{4,3,2,1,0:T(2,128)(2,1)}, u32[]{:S(2)}) %copy-start.2) | copy-done | bytes 6291480
  3.6 0.7 copy-done.5
  4.3 3.4 %shard_map.82 = bf16[4,4,384,256]{3,2,1,0:T(8,128)(2,1)S(1)} custom-call(s32[1,3]{1,0:T(1,128)S(1)} %copy-done.5, s32[2]{0:T(128)S(1)} %pad_add_fusion.me_ref, s32[3,4,1,384]{3,2,1,0:T(1,128)S(1)} %reshape.16.shift_ref, bf16[1536,2,1024]{2,1,0:T(2,128)(2,1)S(1)} %bitcast.6), custom_call_target="tpu_custom_call" | custom-call | tf_op jit(solution)/shard_map/pallas_call | solution.py:60
  7.7 0.0 copy-start.1
  7.7 1.6 %copy-done.1 = bf16[4,4,384,256]{3,2,1,0:T(8,128)(2,1)} copy-done((bf16[4,4,384,256]{3,2,1,0:T(8,128)(2,1)}, bf16[4,4,384,256]{3,2,1,0:T(8,128)(2,1)S(1)}, u32[]{:S(2)}) %copy-start.1) | copy-done | bytes 3145752
  9.3 6.1 %all-to-all-start = ((bf16[4,4,384,256]{3,2,1,0:T(8,128)(2,1)}), bf16[4,4,384,256]{3,2,1,0:T(8,128)(2,1)S(1)}, u32[]{:S(2)}, u32[]{:S(2)}) async-start(bf16[4,4,384,256]{3,2,1,0:T(8,128)(2,1)} %copy-done.1), calls=%async_computation | async-start | bytes 6291456 | tf_op jit(solution)/shard_map/all_to_all | solution.py:356
  15.4 0.0 copy-done.8
  15.4 0.1 copy.15
  15.5 0.1 reshape.17
  15.6 0.0 copy-done.7
  15.6 0.8 copy.12.src_ref
  16.4 0.0 copy-done.9
  16.4 0.8 broadcast_in_dim.4.len_ref
  17.2 0.0 copy-done.6
  17.2 0.8 copy.14.coul_ref
  18.0 13.2 %shard_map.83 = (bf16[384,2432]{1,0:T(8,128)(2,1)}, f32[384,8,256]{2,1,0:T(8,128)}) custom-call(s32[384,16]{1,0:T(8,128)} %copy.12.src_ref, s32[384,1]{1,0:T(8,128)} %broadcast_in_dim.4.len_ref, f32[384,64]{1,0:T(8,128)} %copy.14.coul_ref), custom_call_target="tpu_custom_call" | custom-call | tf_op jit(solution)/shard_map/pallas_call | solution.py:155
  31.2 4.9 %all-to-all-done.x_ref = bf16[4,4,384,256]{3,2,1,0:T(8,128)(2,1)S(1)} async-done(((bf16[4,4,384,256]{3,2,1,0:T(8,128)(2,1)}), bf16[4,4,384,256]{3,2,1,0:T(8,128)(2,1)S(1)}, u32[]{:S(2)}, u32[]{:S(2)}) %all-to-all-start) | async-done | bytes 3145760 | tf_op jit(solution)/shard_map/all_to_all | solution.py:356
  36.1 1.6 %shard_map.84 = (bf16[384,256]{1,0:T(8,128)(2,1)S(1)}, bf16[384,256]{1,0:T(8,128)(2,1)}, bf16[384,256]{1,0:T(8,128)(2,1)}, bf16[384,256]{1,0:T(8,128)(2,1)S(1)}) custom-call(bf16[4,4,384,256]{3,2,1,0:T(8,128)(2,1)S(1)} %all-to-all-done.x_ref), custom_call_target="tpu_custom_call" | custom-call | tf_op jit(solution)/shard_map/pallas_call | solution.py:86
  37.6 2.1 %collective-permute-start = (bf16[384,256]{1,0:T(8,128)(2,1)}, bf16[384,256]{1,0:T(8,128)(2,1)S(1)}, u32[]{:S(2)}, u32[]{:S(2)}) collective-permute-start(bf16[384,256]{1,0:T(8,128)(2,1)} %get-tuple-element.40), channel_id=1, source_target_pairs={{0,2},{1,3},{2,0},{3,1},{4,132},{5,133},{6,134},{7,135},{8,10},{9,... | collective-permute-start | bytes 589832 | tf_op jit(solution)/shard_map/ppermute | solution.py:366
  39.7 0.7 collective-permute-start.1
  40.4 2.6 %collective-permute-start.2 = (bf16[384,256]{1,0:T(8,128)(2,1)S(1)}, bf16[384,256]{1,0:T(8,128)(2,1)S(1)}, u32[]{:S(2)}, u32[]{:S(2)}) collective-permute-start(bf16[384,256]{1,0:T(8,128)(2,1)S(1)} %get-tuple-element.42), channel_id=1, source_target_pairs={{0,3},{1,0},{2,1},{3,2},{4,196},{5,197},{6,198},{7,199},{8,11},{9,... | collective-permute-start | bytes 589832 | tf_op jit(solution)/shard_map/ppermute | solution.py:366
  43.0 0.4 copy.16.rows_ref
  43.3 1.7 %collective-permute-done.a_ref = bf16[384,256]{1,0:T(8,128)(2,1)S(1)} collective-permute-done((bf16[384,256]{1,0:T(8,128)(2,1)}, bf16[384,256]{1,0:T(8,128)(2,1)S(1)}, u32[]{:S(2)}, u32[]{:S(2)}) %collective-permute-start) | collective-permute-done | bytes 196640 | tf_op jit(solution)/shard_map/ppermute | solution.py:366
  45.1 2.1 %collective-permute-done.1.b_ref = bf16[384,256]{1,0:T(8,128)(2,1)S(1)} collective-permute-done((bf16[384,256]{1,0:T(8,128)(2,1)}, bf16[384,256]{1,0:T(8,128)(2,1)S(1)}, u32[]{:S(2)}, u32[]{:S(2)}) %collective-permute-start.1) | collective-permute-done | bytes 196640 | tf_op jit(solution)/shard_map/ppermute | solution.py:366
  47.1 0.0 collective-permute-done.2.c_ref
  47.1 1.7 %shard_map.85 = (bf16[384,256]{1,0:T(8,128)(2,1)S(1)}, bf16[2048,256]{1,0:T(8,128)(2,1)}) custom-call(s32[2048,1]{1,0:T(8,128)S(1)} %copy.16.rows_ref, bf16[384,256]{1,0:T(8,128)(2,1)S(1)} %get-tuple-element.39.own_ref, bf16[384,256]{1,0:T(8,128)(2,1)S(1)} %collective-permute-done.a_ref, bf16[384,256]{1,0:T(8,128)(2,1)S(1)} %collective-permute-done.1.b_ref, ...), custom_call_target="tpu_custom_call" | custom-call | tf_op jit(solution)/shard_map/pallas_call | solution.py:190
  48.9 10.8 %all-to-all-start.1 = ((bf16[64,32,256]{2,1,0:T(8,128)(2,1)}), bf16[64,32,256]{2,1,0:T(8,128)(2,1)S(1)}, u32[]{:S(2)}, u32[]{:S(2)}) async-start(bf16[64,32,256]{2,1,0:T(8,128)(2,1)} %bitcast.4), calls=%async_computation.1 | async-start | bytes 2097152 | tf_op jit(solution)/shard_map/all_to_all | solution.py:371
  59.6 0.0 copy-start.4
  59.7 24.4 %shard_map.86.refs_1_ = bf16[32,256,256]{2,1,0:T(8,128)(2,1)} custom-call(bf16[32,64,1024]{2,1,0:T(8,128)(2,1)} %x_ref), custom_call_target="tpu_custom_call" | custom-call | tf_op jit(solution)/shard_map/pallas_call | solution.py:120
  84.0 2.8 %all-to-all-done.1 = bf16[64,32,256]{2,1,0:T(8,128)(2,1)S(1)} async-done(((bf16[64,32,256]{2,1,0:T(8,128)(2,1)}), bf16[64,32,256]{2,1,0:T(8,128)(2,1)S(1)}, u32[]{:S(2)}, u32[]{:S(2)}) %all-to-all-start.1) | async-done | bytes 1048608 | tf_op jit(solution)/shard_map/all_to_all | solution.py:371
  86.8 0.7 shard_map.87.refs_3_
  87.5 1.0 collective-permute-start.5
  88.5 3.5 %collective-permute-start.4 = (bf16[384,256]{1,0:T(8,128)(2,1)S(1)}, bf16[384,256]{1,0:T(8,128)(2,1)S(1)}, u32[]{:S(2)}, u32[]{:S(2)}) collective-permute-start(bf16[384,256]{1,0:T(8,128)(2,1)S(1)} %shard_map.87.refs_3_), channel_id=1, source_target_pairs={{0,2},{1,3},{2,0},{3,1},{4,6},{5,7},{6,4},{7,5},{8,10},{9,11},{10,... | collective-permute-start | bytes 589832 | tf_op jit(solution)/shard_map/ppermute | solution.py:331
  92.0 0.0 collective-permute-start.3
  92.0 4.1 %collective-permute-done.5.refs_6_ = bf16[384,256]{1,0:T(8,128)(2,1)S(1)} collective-permute-done((bf16[384,256]{1,0:T(8,128)(2,1)S(1)}, bf16[384,256]{1,0:T(8,128)(2,1)S(1)}, u32[]{:S(2)}, u32[]{:S(2)}) %collective-permute-start.5) | collective-permute-done | bytes 196640 | tf_op jit(solution)/shard_map/ppermute | solution.py:331
  96.1 5.5 %collective-permute-done.4.refs_5_ = bf16[384,256]{1,0:T(8,128)(2,1)S(1)} collective-permute-done((bf16[384,256]{1,0:T(8,128)(2,1)S(1)}, bf16[384,256]{1,0:T(8,128)(2,1)S(1)}, u32[]{:S(2)}, u32[]{:S(2)}) %collective-permute-start.4) | collective-permute-done | bytes 196640 | tf_op jit(solution)/shard_map/ppermute | solution.py:331
  101.6 0.0 collective-permute-done.3.refs_4_
  101.6 2.2 %copy-done = bf16[32,256,256]{2,1,0:T(8,128)(2,1)S(1)} copy-done((bf16[32,256,256]{2,1,0:T(8,128)(2,1)S(1)}, bf16[32,256,256]{2,1,0:T(8,128)(2,1)}, u32[]{:S(2)}) %copy-start) | copy-done | bytes 4194328
  103.8 37.9 %shard_map.88 = (bf16[384,256]{1,0:T(8,128)(2,1)S(1)}, bf16[384,256]{1,0:T(8,128)(2,1)S(1)}, bf16[384,256]{1,0:T(8,128)(2,1)S(1)}, bf16[384,256]{1,0:T(8,128)(2,1)S(1)}) custom-call(s32[1]{0:T(128)} %bitcast.refs_0_, bf16[32,256,256]{2,1,0:T(8,128)(2,1)S(1)} %copy-done, f32[384,8,256]{2,1,0:T(8,128)S(1)} %copy-done.3, ...), custom_call_target="tpu_custom_call" | custom-call | tf_op jit(solution)/shard_map/pallas_call | solution.py:281
  141.7 1.5 collective-permute-start.6
  143.3 2.0 %collective-permute-start.7 = (bf16[384,256]{1,0:T(8,128)(2,1)S(1)}, bf16[384,256]{1,0:T(8,128)(2,1)S(1)}, u32[]{:S(2)}, u32[]{:S(2)}) collective-permute-start(bf16[384,256]{1,0:T(8,128)(2,1)S(1)} %get-tuple-element.53), channel_id=1, source_target_pairs={{0,1},{1,2},{2,3},{3,0},{4,5},{5,6},{6,7},{7,4},{8,9},{9,10},{10,1... | collective-permute-start | bytes 589832 | tf_op jit(solution)/shard_map/ppermute | solution.py:331
  145.3 1.2 collective-permute-start.8
  146.5 4.6 %collective-permute-done.6 = bf16[384,256]{1,0:T(8,128)(2,1)S(1)} collective-permute-done((bf16[384,256]{1,0:T(8,128)(2,1)S(1)}, bf16[384,256]{1,0:T(8,128)(2,1)S(1)}, u32[]{:S(2)}, u32[]{:S(2)}) %collective-permute-start.6) | collective-permute-done | bytes 196640 | tf_op jit(solution)/shard_map/ppermute | solution.py:331
  151.1 3.4 %collective-permute-done.7 = bf16[384,256]{1,0:T(8,128)(2,1)S(1)} collective-permute-done((bf16[384,256]{1,0:T(8,128)(2,1)S(1)}, bf16[384,256]{1,0:T(8,128)(2,1)S(1)}, u32[]{:S(2)}, u32[]{:S(2)}) %collective-permute-start.7) | collective-permute-done | bytes 196640 | tf_op jit(solution)/shard_map/ppermute | solution.py:331
  154.5 0.0 collective-permute-done.8
  154.5 0.8 add_convert_fusion
  (10 shorter events, 0.0 us)
Async XLA Ops:
  0.8 2.8 %copy-start.2 = (bf16[1,4,384,2,1024]{4,3,2,1,0:T(2,128)(2,1)S(1)}, bf16[1,4,384,2,1024]{4,3,2,1,0:T(2,128)(2,1)}, u32[]{:S(2)}) copy-start(bf16[1,4,384,2,1024]{4,3,2,1,0:T(2,128)(2,1)} %param.10) | copy-start | bytes 18874372
  3.6 0.7 copy-start.5
  7.7 1.6 %copy-start.1 = (bf16[4,4,384,256]{3,2,1,0:T(8,128)(2,1)}, bf16[4,4,384,256]{3,2,1,0:T(8,128)(2,1)S(1)}, u32[]{:S(2)}) copy-start(bf16[4,4,384,256]{3,2,1,0:T(8,128)(2,1)S(1)} %shard_map.82) | copy-start | bytes 9437188
  9.3 6.1 %copy-start.8 = (s32[1,64,32]{1,2,0:T(8,128)S(1)}, s32[1,64,32]{1,2,0:T(8,128)}, u32[]{:S(2)}) copy-start(s32[1,64,32]{1,2,0:T(8,128)} %param.13) | copy-start | bytes 24580
  9.3 6.3 %copy-start.7 = (s32[384,16]{0,1:T(8,128)S(1)}, s32[384,16]{0,1:T(8,128)}, u32[]{:S(2)}) copy-start(s32[384,16]{0,1:T(8,128)} %param.14) | copy-start | bytes 73732
  9.3 7.1 %copy-start.9 = (s32[384]{0:T(512)S(1)}, s32[384]{0:T(512)}, u32[]{:S(2)}) copy-start(s32[384]{0:T(512)} %param.15) | copy-start | bytes 4612
  9.3 7.9 %copy-start.6 = (f32[384,64]{0,1:T(8,128)S(1)}, f32[384,64]{0,1:T(8,128)}, u32[]{:S(2)}) copy-start(f32[384,64]{0,1:T(8,128)} %param.12) | copy-start | bytes 294916
  9.3 26.8 %all-to-all-start = ((bf16[4,4,384,256]{3,2,1,0:T(8,128)(2,1)}), bf16[4,4,384,256]{3,2,1,0:T(8,128)(2,1)S(1)}, u32[]{:S(2)}, u32[]{:S(2)}) async-start(bf16[4,4,384,256]{3,2,1,0:T(8,128)(2,1)} %copy-done.1), calls=%async_computation | async-start | bytes 6291456 | tf_op jit(solution)/shard_map/all_to_all | solution.py:356
  37.6 7.4 %collective-permute-start = (bf16[384,256]{1,0:T(8,128)(2,1)}, bf16[384,256]{1,0:T(8,128)(2,1)S(1)}, u32[]{:S(2)}, u32[]{:S(2)}) collective-permute-start(bf16[384,256]{1,0:T(8,128)(2,1)} %get-tuple-element.40), channel_id=1, source_target_pairs={{0,2},{1,3},{2,0},{3,1},{4,132},{5,133},{6,134},{7,135},{8,10},{9,... | collective-permute-start | bytes 589832 | tf_op jit(solution)/shard_map/ppermute | solution.py:366
  39.7 7.4 %collective-permute-start.1 = (bf16[384,256]{1,0:T(8,128)(2,1)}, bf16[384,256]{1,0:T(8,128)(2,1)S(1)}, u32[]{:S(2)}, u32[]{:S(2)}) collective-permute-start(bf16[384,256]{1,0:T(8,128)(2,1)} %get-tuple-element.41), channel_id=1, source_target_pairs={{0,1},{1,2},{2,3},{3,0},{4,68},{5,69},{6,70},{7,71},{8,9},{9,10},{... | collective-permute-start | bytes 589832 | tf_op jit(solution)/shard_map/ppermute | solution.py:366
  40.4 6.7 %collective-permute-start.2 = (bf16[384,256]{1,0:T(8,128)(2,1)S(1)}, bf16[384,256]{1,0:T(8,128)(2,1)S(1)}, u32[]{:S(2)}, u32[]{:S(2)}) collective-permute-start(bf16[384,256]{1,0:T(8,128)(2,1)S(1)} %get-tuple-element.42), channel_id=1, source_target_pairs={{0,3},{1,0},{2,1},{3,2},{4,196},{5,197},{6,198},{7,199},{8,11},{9,... | collective-permute-start | bytes 589832 | tf_op jit(solution)/shard_map/ppermute | solution.py:366
  48.9 37.9 %all-to-all-start.1 = ((bf16[64,32,256]{2,1,0:T(8,128)(2,1)}), bf16[64,32,256]{2,1,0:T(8,128)(2,1)S(1)}, u32[]{:S(2)}, u32[]{:S(2)}) async-start(bf16[64,32,256]{2,1,0:T(8,128)(2,1)} %bitcast.4), calls=%async_computation.1 | async-start | bytes 2097152 | tf_op jit(solution)/shard_map/all_to_all | solution.py:371
  59.6 27.1 %copy-start.4 = (bf16[384,2432]{1,0:T(8,128)(2,1)S(1)}, bf16[384,2432]{1,0:T(8,128)(2,1)}, u32[]{:S(2)}) copy-start(bf16[384,2432]{1,0:T(8,128)(2,1)} %get-tuple-element.48.counts_ref) | copy-start | bytes 5603332
  86.8 14.9 %copy-start.3 = (f32[384,8,256]{2,1,0:T(8,128)S(1)}, f32[384,8,256]{2,1,0:T(8,128)}, u32[]{:S(2)}) copy-start(f32[384,8,256]{2,1,0:T(8,128)} %get-tuple-element.47.refs_2_) | copy-start | bytes 9437188
  87.5 8.6 %collective-permute-start.5 = (bf16[384,256]{1,0:T(8,128)(2,1)S(1)}, bf16[384,256]{1,0:T(8,128)(2,1)S(1)}, u32[]{:S(2)}, u32[]{:S(2)}) collective-permute-start(bf16[384,256]{1,0:T(8,128)(2,1)S(1)} %shard_map.87.refs_3_), channel_id=1, source_target_pairs={{0,1},{1,2},{2,3},{3,0},{4,5},{5,6},{6,7},{7,4},{8,9},{9,10},{10,1... | collective-permute-start | bytes 589832 | tf_op jit(solution)/shard_map/ppermute | solution.py:331
  88.5 13.1 %collective-permute-start.4 = (bf16[384,256]{1,0:T(8,128)(2,1)S(1)}, bf16[384,256]{1,0:T(8,128)(2,1)S(1)}, u32[]{:S(2)}, u32[]{:S(2)}) collective-permute-start(bf16[384,256]{1,0:T(8,128)(2,1)S(1)} %shard_map.87.refs_3_), channel_id=1, source_target_pairs={{0,2},{1,3},{2,0},{3,1},{4,6},{5,7},{6,4},{7,5},{8,10},{9,11},{10,... | collective-permute-start | bytes 589832 | tf_op jit(solution)/shard_map/ppermute | solution.py:331
  92.0 9.6 %collective-permute-start.3 = (bf16[384,256]{1,0:T(8,128)(2,1)S(1)}, bf16[384,256]{1,0:T(8,128)(2,1)S(1)}, u32[]{:S(2)}, u32[]{:S(2)}) collective-permute-start(bf16[384,256]{1,0:T(8,128)(2,1)S(1)} %shard_map.87.refs_3_), channel_id=1, source_target_pairs={{0,3},{1,0},{2,1},{3,2},{4,7},{5,4},{6,5},{7,6},{8,11},{9,8},{10,9... | collective-permute-start | bytes 589832 | tf_op jit(solution)/shard_map/ppermute | solution.py:331
  101.6 2.2 %copy-start = (bf16[32,256,256]{2,1,0:T(8,128)(2,1)S(1)}, bf16[32,256,256]{2,1,0:T(8,128)(2,1)}, u32[]{:S(2)}) copy-start(bf16[32,256,256]{2,1,0:T(8,128)(2,1)} %shard_map.86.refs_1_) | copy-start | bytes 12582916
  141.7 9.4 %collective-permute-start.6 = (bf16[384,256]{1,0:T(8,128)(2,1)S(1)}, bf16[384,256]{1,0:T(8,128)(2,1)S(1)}, u32[]{:S(2)}, u32[]{:S(2)}) collective-permute-start(bf16[384,256]{1,0:T(8,128)(2,1)S(1)} %get-tuple-element.52), channel_id=1, source_target_pairs={{0,2},{1,3},{2,0},{3,1},{4,6},{5,7},{6,4},{7,5},{8,10},{9,11},{10,... | collective-permute-start | bytes 589832 | tf_op jit(solution)/shard_map/ppermute | solution.py:331
  143.3 11.3 %collective-permute-start.7 = (bf16[384,256]{1,0:T(8,128)(2,1)S(1)}, bf16[384,256]{1,0:T(8,128)(2,1)S(1)}, u32[]{:S(2)}, u32[]{:S(2)}) collective-permute-start(bf16[384,256]{1,0:T(8,128)(2,1)S(1)} %get-tuple-element.53), channel_id=1, source_target_pairs={{0,1},{1,2},{2,3},{3,0},{4,5},{5,6},{6,7},{7,4},{8,9},{9,10},{10,1... | collective-permute-start | bytes 589832 | tf_op jit(solution)/shard_map/ppermute | solution.py:331
  145.3 9.2 %collective-permute-start.8 = (bf16[384,256]{1,0:T(8,128)(2,1)S(1)}, bf16[384,256]{1,0:T(8,128)(2,1)S(1)}, u32[]{:S(2)}, u32[]{:S(2)}) collective-permute-start(bf16[384,256]{1,0:T(8,128)(2,1)S(1)} %get-tuple-element.54), channel_id=1, source_target_pairs={{0,3},{1,0},{2,1},{3,2},{4,7},{5,4},{6,5},{7,6},{8,11},{9,8},{10,9... | collective-permute-start | bytes 589832 | tf_op jit(solution)/shard_map/ppermute | solution.py:331

commit v3 on v2

--- a/solution.py
+++ b/solution.py
@@ -13,6 +13,7 @@
 ROWS = 128
 GROUP = 4
 QUARTERS = 4
+FULL = 60 * 2**20
 AXES = ("ka", "pair", "aux")
 F32 = jnp.float32
 BF16 = jnp.bfloat16
@@ -24,18 +25,26 @@
     return lax.broadcasted_iota(jnp.int32, shape, dim)
 
 
-def term_kernel(kp_ref, me_ref, shift_ref, x_ref, o_ref):
+def term_kernel(kp_ref, shift_ref, x_ref, o_ref, stage, sem):
     g = pl.program_id(0)
     rows, _, width = x_ref.shape
     turns = (
-        kp_ref[0, 0] * (NK // 4) * shift_ref[0, 0]
-        + kp_ref[0, 1] * (NK // 2) * shift_ref[1, 0]
-        + kp_ref[0, 2] * (NK // 2) * shift_ref[2, 0]
+        kp_ref[0, 0] * (NK // 4) * shift_ref[0, pl.ds(g, 1)]
+        + kp_ref[0, 1] * (NK // 2) * shift_ref[1, pl.ds(g, 1)]
+        + kp_ref[0, 2] * (NK // 2) * shift_ref[2, pl.ds(g, 1)]
     ) & (NK - 1)
     angle = turns.astype(F32) * (2.0 * math.pi / NK)
     even, odd = jnp.cos(angle) / NK, jnp.sin(angle) / NK
     row, col = iota((2 * ROWS, ROWS), 0), iota((2 * ROWS, ROWS), 1)
-    core, second = me_ref[0], me_ref[1]
+    core = lax.axis_index("pair") % 2
+    second = jnp.where(core == 0, lax.axis_index("aux"), lax.axis_index("ka"))
+    pieces = width // WIDE
+
+    def copy_out(slab, j):
+        first = jnp.where(core == 0, slab, j)
+        other = (jnp.where(core == 0, j, slab) - second) & 3
+        return pltpu.make_async_copy(stage.at[slab, j], o_ref.at[first, other], sem.at[slab, j])
+
     for i in range(rows // ROWS):
         here = slice(i * ROWS, (i + 1) * ROWS)
         phase = jnp.where(
@@ -47,13 +56,19 @@
         block = x_ref[here].reshape(2 * ROWS, width)
         term = jnp.dot(both, block, preferred_element_type=F32)
         term = (term[:ROWS] + term[ROWS:]).astype(BF16)
-        for j in range(width // WIDE):
-            first = jnp.where(core == 0, g, j)
-            other = (jnp.where(core == 0, j, g) - second) & 3
-            o_ref[first, other, here] = term[:, WIDE * j : WIDE * (j + 1)]
-
-
-def kpoint_terms(kpoint, me, shift, block):
+        for j in range(pieces):
+            stage[g, j, here] = term[:, WIDE * j : WIDE * (j + 1)]
+    for j in range(pieces):
+        copy_out(g, j).start()
+
+    @pl.when(g == stage.shape[0] - 1)
+    def _():
+        for slab in range(stage.shape[0]):
+            for j in range(pieces):
+                copy_out(slab, j).wait()
+
+
+def kpoint_terms(kpoint, shift, block):
     slabs, rows = block.shape[:2]
     width = block.shape[-1]
     shape = (slabs, width // WIDE, rows, WIDE)
@@ -62,14 +77,14 @@
         grid=(slabs,),
         in_specs=[
             pl.BlockSpec(memory_space=pltpu.SMEM),
-            pl.BlockSpec(memory_space=pltpu.SMEM),
-            pl.BlockSpec((3, 1, 1, rows), lambda g: (0, g, 0, 0)),
+            pl.BlockSpec((3, slabs, rows), lambda g: (0, 0, 0)),
             pl.BlockSpec((rows, 2, width), lambda g: (g, 0, 0)),
         ],
-        out_specs=pl.BlockSpec(shape, lambda g: (0, 0, 0, 0)),
+        out_specs=pl.BlockSpec(memory_space=pl.ANY),
         out_shape=jax.ShapeDtypeStruct(shape, BF16),
-        compiler_params=pltpu.CompilerParams(vmem_limit_bytes=40 * 2**20),
-    )(kpoint, me, shift.reshape(3, slabs, 1, rows), block.reshape(slabs * rows, 2, width))
+        scratch_shapes=[pltpu.VMEM(shape, BF16), pltpu.SemaphoreType.DMA(shape[:2])],
+        compiler_params=pltpu.CompilerParams(vmem_limit_bytes=FULL),
+    )(kpoint, shift, block.reshape(slabs * rows, 2, width))
 
 
 def half_sum_kernel(x_ref, *o_refs):
@@ -214,55 +229,76 @@
 
 def exchange_kernel(pairs_atom, me_ref, c_ref, w_ref, *refs):
     y_refs, o_refs = refs[:QUARTERS], refs[QUARTERS : 2 * QUARTERS]
-    y_all, y_rows, weighted, folded, gather, diag = refs[2 * QUARTERS :]
+    y_all, y_rows, even, odd, folded, gather, diag = refs[2 * QUARTERS :]
     atoms = c_ref.shape[0]
     targets = atoms * pairs_atom
     me = me_ref[0]
 
     @pl.when(pl.program_id(0) == 0)
     def _():
-        shape = (QUARTERS * targets, targets * NB)
+        shape = (targets, targets * NB)
         row, col = iota(shape, 0), iota(shape, 1)
-        quarter = (row // targets + me) & 3
-        keep = (row % targets == col // NB) & (quarter == (col % NB) // 8)
-        gather[...] = keep.astype(F32).astype(BF16)
+        for r in range(QUARTERS):
+            keep = (row == col // NB) & (((me + r) & 3) == (col % NB) // 8)
+            gather[r * targets : (r + 1) * targets] = keep.astype(F32).astype(BF16)
         square = (WIDE, WIDE)
         diag[...] = (iota(square, 0) // NB == iota(square, 1) // NB).astype(F32).astype(BF16)
 
-    square = (WIDE, WIDE)
+    lanes = WIDE // 2
+    square = (lanes, lanes)
     fold = (iota(square, 0) % NB == iota(square, 1) % NB).astype(F32).astype(BF16)
-    spread = (targets, 8, WIDE)
-    keep = iota(spread, 2) // NB == iota(spread, 1)
+    spread = (targets, 8, lanes)
+    low = iota(spread, 2) // NB == iota(spread, 1)
+    high = iota(spread, 2) // NB + 4 == iota(spread, 1)
     for r, y_ref in enumerate(y_refs):
         y_all[(me + r) & 3] = y_ref[...].astype(F32)
     parts = []
     for j in range(QUARTERS):
-        parts.append(jnp.where(keep, jnp.broadcast_to(y_all[j][:, None, :], spread), 0.0))
-    rows = jnp.concatenate(parts, axis=1).reshape(targets * NB, WIDE).astype(BF16)
-    y_rows[...] = jnp.dot(rows, fold, preferred_element_type=F32).astype(BF16)
+        y = y_all[j]
+        left = jnp.broadcast_to(y[:, None, :lanes], spread)
+        right = jnp.broadcast_to(y[:, None, lanes:], spread)
+        parts.append(jnp.where(low, left, jnp.where(high, right, 0.0)))
+    rows = jnp.concatenate(parts, axis=1).reshape(targets * NB, lanes).astype(BF16)
+    rows = jnp.dot(rows, fold, preferred_element_type=F32).astype(BF16)
+    y_rows[:, :lanes] = rows
+    y_rows[:, lanes:] = rows
     tall = (pairs_atom * NB, WIDE)
     keep_out = iota(tall, 0) % 8 == iota(tall, 1) // NB
 
-    def atom(a, carry):
+    halves = 2
+    chunks = 8 // halves
+
+    def first(a, t):
+        target = a * pairs_atom + t
+        y = y_rows[target * NB : (target + 1) * NB, :]
+        y = jnp.concatenate([y] * 8, axis=0) * diag[...]
+        inner = jnp.dot(c_ref[a], y, preferred_element_type=F32)
+        inner = inner.reshape(8, NB, WIDE) * w_ref[target][:, None, :]
+        inner = inner.astype(BF16)
+        weighted = (even, odd)[a % 2]
+        for p in range(8):
+            weighted[t * NB : (t + 1) * NB, WIDE * p : WIDE * (p + 1)] = inner[p]
+
+    def second(a, half):
         c = c_ref[a]
+        chunk = range(half * chunks, (half + 1) * chunks)
+        flat = jnp.concatenate([c[NB * p : NB * (p + 1), :] for p in chunk], axis=1)
+        flat = jnp.concatenate([flat] * 8, axis=0)
+        lanes_here = slice(half * chunks * WIDE, (half + 1) * chunks * WIDE)
+        weighted = (even, odd)[a % 2][:, lanes_here]
+        return lax.dot_general(weighted, flat, NT, preferred_element_type=F32)
+
+    for a in range(atoms + 1):
+        total = None
         for t in range(pairs_atom):
-            target = a * pairs_atom + t
-            y = y_rows[pl.ds(pl.multiple_of(target * NB, NB), NB), :]
-            y = jnp.concatenate([y] * 8, axis=0) * diag[...]
-            inner = jnp.dot(c, y, preferred_element_type=F32)
-            inner = inner.reshape(8, NB, WIDE) * w_ref[target][:, None, :]
-            inner = inner.astype(BF16)
-            for p in range(8):
-                weighted[p, t * NB : (t + 1) * NB, :] = inner[p]
-        total = jnp.zeros(tall, F32)
-        for p in range(8):
-            copies = jnp.concatenate([c[NB * p : NB * (p + 1), :]] * 8, axis=0)
-            total += lax.dot_general(weighted[p], copies, NT, preferred_element_type=F32)
-        start = pl.multiple_of(a * pairs_atom * NB, 128)
-        folded[pl.ds(start, pairs_atom * NB), :] = jnp.where(keep_out, total, 0.0).astype(BF16)
-        return carry
-
-    lax.fori_loop(0, atoms, atom, 0)
+            if a < atoms:
+                first(a, t)
+            if a > 0 and (t + 1) % (pairs_atom // halves) == 0:
+                part = second(a - 1, t // (pairs_atom // halves))
+                total = part if total is None else total + part
+        if a > 0:
+            here = slice((a - 1) * pairs_atom * NB, a * pairs_atom * NB)
+            folded[here] = jnp.where(keep_out, total, 0.0).astype(BF16)
     result = jnp.dot(gather[...], folded[...], preferred_element_type=F32).astype(BF16)
     for r, o_ref in enumerate(o_refs):
         o_ref[...] = result[r * targets : (r + 1) * targets]
@@ -292,12 +328,13 @@
         scratch_shapes=[
             pltpu.VMEM((QUARTERS, step, WIDE), F32),
             pltpu.VMEM((step * NB, WIDE), BF16),
-            pltpu.VMEM((8, pairs_atom * NB, WIDE), BF16),
+            pltpu.VMEM((pairs_atom * NB, 8 * WIDE), BF16),
+            pltpu.VMEM((pairs_atom * NB, 8 * WIDE), BF16),
             pltpu.VMEM((step * NB, WIDE), BF16),
             pltpu.VMEM((QUARTERS * step, step * NB), BF16),
             pltpu.VMEM((WIDE, WIDE), BF16),
         ],
-        compiler_params=pltpu.CompilerParams(vmem_limit_bytes=40 * 2**20),
+        compiler_params=pltpu.CompilerParams(vmem_limit_bytes=FULL),
     )(me, coeff, weights, *quarters)
 
 
@@ -344,12 +381,9 @@
     ):
         targets = coulomb.shape[0]
         slots = send_rows.shape[1] * send_rows.shape[2]
-        core = lax.axis_index("pair") % 2
         aux = lax.axis_index("aux")
-        second = jnp.where(core == 0, aux, lax.axis_index("ka"))
-        me = jnp.stack([core, second]).astype(jnp.int32)
-
-        terms = kpoint_terms(kpoint_grid, me, image_shift, density_k[0])
+
+        terms = kpoint_terms(kpoint_grid, image_shift, density_k[0])
         terms, coulomb, source_index, list_length, send_rows = lax.optimization_barrier(
             (terms, coulomb, source_index, list_length, send_rows)
         )

time: 158 us -> 150 us (0.949)
  local copies, waits for them, and re-layouts: 10.9 us -> 3.7 us
  Pallas kernels: 82.9 us -> 80.9 us
    unnamed x20 -> x18, local copies, waits for them, and re-layouts: 7.27 us -> 0.77 us
    pallas_call x1, Pallas kernels: 37.9 us -> 33 us  [exchange(): pl.pallas_call(kernel, grid=(atoms // GROUP,), in_specs=[pl.BlockSpec(mem...]
    pallas_call x1, Pallas kernels: 3.41 us -> 6.44 us  [kpoint_terms(): pl.pallas_call(term_kernel, grid=(slabs,), in_specs=[pl.BlockSpec(memory_...]
  transfers between devices with their start and end apart: 11 -> 11, of which waited for: 8 -> 8; matrix products, arithmetic and copies ran while one was open for 2% -> 2% of each run, Pallas kernels for 24% -> 26%
where the time goes in v3:
time: 150 us; the launch traced here: 147 us
  Pallas kernels  80.9 us (54%)
  starting transfers between devices  31.5 us (21%)
  waiting for transfers between devices  29.3 us (20%)
  local copies, waits for them, and re-layouts  3.7 us (2%)
  other arithmetic  1.71 us (1%)
    pallas_call x1, Pallas kernels, exchange(): pl.pallas_call(kernel, grid=(atoms // GROUP,), in_specs=[pl.BlockSpec(mem...  33 us
    pallas_call x1, Pallas kernels, relay_coefficients(): pl.pallas_call(relay_kernel, grid=(atoms,), in_specs=[pl.BlockSpec((1, au...  24.4 us
    ppermute x6, waiting for transfers between devices, along_aux(): lax.ppermute(array, 'aux', [(i, (i + by) % QUARTERS) for i in range(QUART...  17.9 us
    pallas_call x1, Pallas kernels, entry_counts(): pl.pallas_call(count_kernel, grid=(targets // step,), in_specs=[pl.BlockS...  13.2 us
    all_to_all x1, starting transfers between devices, shards(): lax.all_to_all(sent, ('ka', 'pair'), split_axis=0, concat_axis=0, tiled=T...  10.8 us
    ppermute x6, starting transfers between devices, along_aux(): lax.ppermute(array, 'aux', [(i, (i + by) % QUARTERS) for i in range(QUART...  9.28 us
    pallas_call x1, Pallas kernels, kpoint_terms(): pl.pallas_call(term_kernel, grid=(slabs,), in_specs=[pl.BlockSpec(memory_...  6.44 us
    all_to_all x1, starting transfers between devices, shards(): lax.all_to_all(terms, AXES, split_axis=0, concat_axis=0, tiled=True, axis...  6.09 us
  transfers between devices with their start and end apart: 11, of which 8 were waited for; matrix products, arithmetic and copies ran while one was open for 2% of the time, Pallas kernels for 26%

profile of v3, /device:TPU:2, one launch (start us, length us, event | category | flops | bytes accessed | tf_op | source)
XLA Modules:
  0.0 147.2 jit_solution(9800706369679846423)
XLA Ops:
  0.0 6.4 %shard_map.82 = bf16[4,4,384,256]{3,2,1,0:T(8,128)(2,1)} custom-call(s32[1,3]{1,0:T(1,128)} %kp_ref.1, s32[3,4,384]{2,1,0:T(4,128)} %shift_ref.1, bf16[1536,2,1024]{2,1,0:T(2,128)(2,1)} %bitcast.5), custom_call_target="tpu_custom_call" | custom-call | tf_op jit(solution)/shard_map/pallas_call | solution.py:75
  6.5 0.0 copy-start.7
  6.5 0.0 copy-start.6
  6.5 0.0 copy-start.8
  6.5 0.0 copy-start.5
  6.5 6.1 %all-to-all-start = ((bf16[4,4,384,256]{3,2,1,0:T(8,128)(2,1)}), bf16[4,4,384,256]{3,2,1,0:T(8,128)(2,1)S(1)}, u32[]{:S(2)}, u32[]{:S(2)}) async-start(bf16[4,4,384,256]{3,2,1,0:T(8,128)(2,1)} %shard_map.82), calls=%async_computation | async-start | bytes 6291456 | tf_op jit(solution)/shard_map/all_to_all | solution.py:390
  12.6 0.0 copy-done.7
  12.6 0.1 copy.15
  12.7 0.1 reshape.13
  12.8 0.0 copy-done.6
  12.8 0.8 copy.12.src_ref
  13.6 0.0 copy-done.8
  13.6 0.8 broadcast_in_dim.4.len_ref
  14.4 0.0 copy-done.5
  14.4 0.8 copy.14.coul_ref
  15.2 13.2 %shard_map.83 = (bf16[384,2432]{1,0:T(8,128)(2,1)}, f32[384,8,256]{2,1,0:T(8,128)}) custom-call(s32[384,16]{1,0:T(8,128)} %copy.12.src_ref, s32[384,1]{1,0:T(8,128)} %broadcast_in_dim.4.len_ref, f32[384,64]{1,0:T(8,128)} %copy.14.coul_ref), custom_call_target="tpu_custom_call" | custom-call | tf_op jit(solution)/shard_map/pallas_call | solution.py:170
  28.4 4.9 %all-to-all-done.x_ref = bf16[4,4,384,256]{3,2,1,0:T(8,128)(2,1)S(1)} async-done(((bf16[4,4,384,256]{3,2,1,0:T(8,128)(2,1)}), bf16[4,4,384,256]{3,2,1,0:T(8,128)(2,1)S(1)}, u32[]{:S(2)}, u32[]{:S(2)}) %all-to-all-start) | async-done | bytes 3145760 | tf_op jit(solution)/shard_map/all_to_all | solution.py:390
  33.3 1.6 %shard_map.84 = (bf16[384,256]{1,0:T(8,128)(2,1)S(1)}, bf16[384,256]{1,0:T(8,128)(2,1)}, bf16[384,256]{1,0:T(8,128)(2,1)}, bf16[384,256]{1,0:T(8,128)(2,1)S(1)}) custom-call(bf16[4,4,384,256]{3,2,1,0:T(8,128)(2,1)S(1)} %all-to-all-done.x_ref), custom_call_target="tpu_custom_call" | custom-call | tf_op jit(solution)/shard_map/pallas_call | solution.py:101
  34.8 2.1 %collective-permute-start = (bf16[384,256]{1,0:T(8,128)(2,1)}, bf16[384,256]{1,0:T(8,128)(2,1)S(1)}, u32[]{:S(2)}, u32[]{:S(2)}) collective-permute-start(bf16[384,256]{1,0:T(8,128)(2,1)} %get-tuple-element.40), channel_id=1, source_target_pairs={{0,2},{1,3},{2,0},{3,1},{4,132},{5,133},{6,134},{7,135},{8,10},{9,... | collective-permute-start | bytes 589832 | tf_op jit(solution)/shard_map/ppermute | solution.py:400
  36.9 0.7 collective-permute-start.1
  37.6 2.6 %collective-permute-start.2 = (bf16[384,256]{1,0:T(8,128)(2,1)S(1)}, bf16[384,256]{1,0:T(8,128)(2,1)S(1)}, u32[]{:S(2)}, u32[]{:S(2)}) collective-permute-start(bf16[384,256]{1,0:T(8,128)(2,1)S(1)} %get-tuple-element.42), channel_id=1, source_target_pairs={{0,3},{1,0},{2,1},{3,2},{4,196},{5,197},{6,198},{7,199},{8,11},{9,... | collective-permute-start | bytes 589832 | tf_op jit(solution)/shard_map/ppermute | solution.py:400
  40.1 0.4 copy.16.rows_ref
  40.5 1.7 %collective-permute-done.a_ref = bf16[384,256]{1,0:T(8,128)(2,1)S(1)} collective-permute-done((bf16[384,256]{1,0:T(8,128)(2,1)}, bf16[384,256]{1,0:T(8,128)(2,1)S(1)}, u32[]{:S(2)}, u32[]{:S(2)}) %collective-permute-start) | collective-permute-done | bytes 196640 | tf_op jit(solution)/shard_map/ppermute | solution.py:400
  42.2 2.1 %collective-permute-done.1.b_ref = bf16[384,256]{1,0:T(8,128)(2,1)S(1)} collective-permute-done((bf16[384,256]{1,0:T(8,128)(2,1)}, bf16[384,256]{1,0:T(8,128)(2,1)S(1)}, u32[]{:S(2)}, u32[]{:S(2)}) %collective-permute-start.1) | collective-permute-done | bytes 196640 | tf_op jit(solution)/shard_map/ppermute | solution.py:400
  44.3 0.0 collective-permute-done.2.c_ref
  44.3 1.7 %shard_map.85 = (bf16[384,256]{1,0:T(8,128)(2,1)S(1)}, bf16[2048,256]{1,0:T(8,128)(2,1)}) custom-call(s32[2048,1]{1,0:T(8,128)S(1)} %copy.16.rows_ref, bf16[384,256]{1,0:T(8,128)(2,1)S(1)} %get-tuple-element.39.own_ref, bf16[384,256]{1,0:T(8,128)(2,1)S(1)} %collective-permute-done.a_ref, bf16[384,256]{1,0:T(8,128)(2,1)S(1)} %collective-permute-done.1.b_ref, ...), custom_call_target="tpu_custom_call" | custom-call | tf_op jit(solution)/shard_map/pallas_call | solution.py:205
  46.0 10.8 %all-to-all-start.1 = ((bf16[64,32,256]{2,1,0:T(8,128)(2,1)}), bf16[64,32,256]{2,1,0:T(8,128)(2,1)S(1)}, u32[]{:S(2)}, u32[]{:S(2)}) async-start(bf16[64,32,256]{2,1,0:T(8,128)(2,1)} %bitcast.2), calls=%async_computation.1 | async-start | bytes 2097152 | tf_op jit(solution)/shard_map/all_to_all | solution.py:405
  56.8 24.4 %shard_map.86.refs_1_ = bf16[32,256,256]{2,1,0:T(8,128)(2,1)} custom-call(bf16[32,64,1024]{2,1,0:T(8,128)(2,1)} %x_ref), custom_call_target="tpu_custom_call" | custom-call | tf_op jit(solution)/shard_map/pallas_call | solution.py:135
  81.2 2.8 %all-to-all-done.1 = bf16[64,32,256]{2,1,0:T(8,128)(2,1)S(1)} async-done(((bf16[64,32,256]{2,1,0:T(8,128)(2,1)}), bf16[64,32,256]{2,1,0:T(8,128)(2,1)S(1)}, u32[]{:S(2)}, u32[]{:S(2)}) %all-to-all-start.1) | async-done | bytes 1048608 | tf_op jit(solution)/shard_map/all_to_all | solution.py:405
  83.9 0.7 shard_map.87.refs_3_
  84.6 0.0 copy-start.1
  84.6 1.0 collective-permute-start.5
  85.6 3.5 %collective-permute-start.4 = (bf16[384,256]{1,0:T(8,128)(2,1)S(1)}, bf16[384,256]{1,0:T(8,128)(2,1)S(1)}, u32[]{:S(2)}, u32[]{:S(2)}) collective-permute-start(bf16[384,256]{1,0:T(8,128)(2,1)S(1)} %shard_map.87.refs_3_), channel_id=1, source_target_pairs={{0,2},{1,3},{2,0},{3,1},{4,6},{5,7},{6,4},{7,5},{8,10},{9,11},{10,... | collective-permute-start | bytes 589832 | tf_op jit(solution)/shard_map/ppermute | solution.py:368
  89.2 0.0 collective-permute-start.3
  89.2 4.1 %collective-permute-done.5.refs_6_ = bf16[384,256]{1,0:T(8,128)(2,1)S(1)} collective-permute-done((bf16[384,256]{1,0:T(8,128)(2,1)S(1)}, bf16[384,256]{1,0:T(8,128)(2,1)S(1)}, u32[]{:S(2)}, u32[]{:S(2)}) %collective-permute-start.5) | collective-permute-done | bytes 196640 | tf_op jit(solution)/shard_map/ppermute | solution.py:368
  93.3 5.5 %collective-permute-done.4.refs_5_ = bf16[384,256]{1,0:T(8,128)(2,1)S(1)} collective-permute-done((bf16[384,256]{1,0:T(8,128)(2,1)S(1)}, bf16[384,256]{1,0:T(8,128)(2,1)S(1)}, u32[]{:S(2)}, u32[]{:S(2)}) %collective-permute-start.4) | collective-permute-done | bytes 196640 | tf_op jit(solution)/shard_map/ppermute | solution.py:368
  98.8 0.0 collective-permute-done.3.refs_4_
  98.8 0.0 copy-done.1
  98.8 0.7 copy-done.3
  99.5 0.1 copy-done.4
  99.5 33.0 %shard_map.88 = (bf16[384,256]{1,0:T(8,128)(2,1)}, bf16[384,256]{1,0:T(8,128)(2,1)}, bf16[384,256]{1,0:T(8,128)(2,1)}, bf16[384,256]{1,0:T(8,128)(2,1)}) custom-call(s32[1]{0:T(128)} %bitcast.refs_0_, bf16[32,256,256]{2,1,0:T(8,128)(2,1)} %shard_map.86.refs_1_, f32[384,8,256]{2,1,0:T(8,128)} %get-tuple-element.47.refs_2_, bf16[384,256]{1,0:T(8,128)(2,1)} %copy-done.1, ...), custom_call_target="tpu_custom_call" | custom-call | tf_op jit(solution)/shard_map/pallas_call | solution.py:317
  132.5 1.5 %collective-permute-start.6 = (bf16[384,256]{1,0:T(8,128)(2,1)}, bf16[384,256]{1,0:T(8,128)(2,1)S(1)}, u32[]{:S(2)}, u32[]{:S(2)}) collective-permute-start(bf16[384,256]{1,0:T(8,128)(2,1)} %get-tuple-element.52), channel_id=1, source_target_pairs={{0,2},{1,3},{2,0},{3,1},{4,6},{5,7},{6,4},{7,5},{8,10},{9,11},{10,... | collective-permute-start | bytes 589832 | tf_op jit(solution)/shard_map/ppermute | solution.py:368
  134.0 2.0 %collective-permute-start.7 = (bf16[384,256]{1,0:T(8,128)(2,1)}, bf16[384,256]{1,0:T(8,128)(2,1)S(1)}, u32[]{:S(2)}, u32[]{:S(2)}) collective-permute-start(bf16[384,256]{1,0:T(8,128)(2,1)} %get-tuple-element.53), channel_id=1, source_target_pairs={{0,1},{1,2},{2,3},{3,0},{4,5},{5,6},{6,7},{7,4},{8,9},{9,10},{10,1... | collective-permute-start | bytes 589832 | tf_op jit(solution)/shard_map/ppermute | solution.py:368
  136.0 1.2 collective-permute-start.8
  137.3 4.9 %collective-permute-done.6 = bf16[384,256]{1,0:T(8,128)(2,1)S(1)} collective-permute-done((bf16[384,256]{1,0:T(8,128)(2,1)}, bf16[384,256]{1,0:T(8,128)(2,1)S(1)}, u32[]{:S(2)}, u32[]{:S(2)}) %collective-permute-start.6) | collective-permute-done | bytes 196640 | tf_op jit(solution)/shard_map/ppermute | solution.py:368
  142.1 3.4 %collective-permute-done.7 = bf16[384,256]{1,0:T(8,128)(2,1)S(1)} collective-permute-done((bf16[384,256]{1,0:T(8,128)(2,1)}, bf16[384,256]{1,0:T(8,128)(2,1)S(1)}, u32[]{:S(2)}, u32[]{:S(2)}) %collective-permute-start.7) | collective-permute-done | bytes 196640 | tf_op jit(solution)/shard_map/ppermute | solution.py:368
  145.5 0.0 collective-permute-done.8
  145.5 1.7 %add_convert_fusion = bf16[384,256]{1,0:T(8,128)(2,1)} fusion(bf16[384,256]{1,0:T(8,128)(2,1)S(1)} %collective-permute-done.8, bf16[384,256]{1,0:T(8,128)(2,1)S(1)} %collective-permute-done.7, bf16[384,256]{1,0:T(8,128)(2,1)S(1)} %collective-permute-done.6, bf16[384,256]{1,0:T(8,128)(2,1)} %get-tuple-element.51), kind=kLoop, calls=%fused_computation | loop fusion | flops 786432 | bytes 983040 | tf_op jit(solution)/shard_map/convert_element_type | solution.py:413
  (6 shorter events, 0.0 us)
Async XLA Ops:
  6.5 6.1 %copy-start.7 = (s32[1,64,32]{1,2,0:T(8,128)S(1)}, s32[1,64,32]{1,2,0:T(8,128)}, u32[]{:S(2)}) copy-start(s32[1,64,32]{1,2,0:T(8,128)} %param.13) | copy-start | bytes 24580
  6.5 6.3 %copy-start.6 = (s32[384,16]{0,1:T(8,128)S(1)}, s32[384,16]{0,1:T(8,128)}, u32[]{:S(2)}) copy-start(s32[384,16]{0,1:T(8,128)} %param.14) | copy-start | bytes 73732
  6.5 7.1 %copy-start.8 = (s32[384]{0:T(512)S(1)}, s32[384]{0:T(512)}, u32[]{:S(2)}) copy-start(s32[384]{0:T(512)} %param.15) | copy-start | bytes 4612
  6.5 7.9 %copy-start.5 = (f32[384,64]{0,1:T(8,128)S(1)}, f32[384,64]{0,1:T(8,128)}, u32[]{:S(2)}) copy-start(f32[384,64]{0,1:T(8,128)} %param.12) | copy-start | bytes 294916
  6.5 26.8 %all-to-all-start = ((bf16[4,4,384,256]{3,2,1,0:T(8,128)(2,1)}), bf16[4,4,384,256]{3,2,1,0:T(8,128)(2,1)S(1)}, u32[]{:S(2)}, u32[]{:S(2)}) async-start(bf16[4,4,384,256]{3,2,1,0:T(8,128)(2,1)} %shard_map.82), calls=%async_computation | async-start | bytes 6291456 | tf_op jit(solution)/shard_map/all_to_all | solution.py:390
  34.8 7.4 %collective-permute-start = (bf16[384,256]{1,0:T(8,128)(2,1)}, bf16[384,256]{1,0:T(8,128)(2,1)S(1)}, u32[]{:S(2)}, u32[]{:S(2)}) collective-permute-start(bf16[384,256]{1,0:T(8,128)(2,1)} %get-tuple-element.40), channel_id=1, source_target_pairs={{0,2},{1,3},{2,0},{3,1},{4,132},{5,133},{6,134},{7,135},{8,10},{9,... | collective-permute-start | bytes 589832 | tf_op jit(solution)/shard_map/ppermute | solution.py:400
  36.9 7.4 %collective-permute-start.1 = (bf16[384,256]{1,0:T(8,128)(2,1)}, bf16[384,256]{1,0:T(8,128)(2,1)S(1)}, u32[]{:S(2)}, u32[]{:S(2)}) collective-permute-start(bf16[384,256]{1,0:T(8,128)(2,1)} %get-tuple-element.41), channel_id=1, source_target_pairs={{0,1},{1,2},{2,3},{3,0},{4,68},{5,69},{6,70},{7,71},{8,9},{9,10},{... | collective-permute-start | bytes 589832 | tf_op jit(solution)/shard_map/ppermute | solution.py:400
  37.6 6.7 %collective-permute-start.2 = (bf16[384,256]{1,0:T(8,128)(2,1)S(1)}, bf16[384,256]{1,0:T(8,128)(2,1)S(1)}, u32[]{:S(2)}, u32[]{:S(2)}) collective-permute-start(bf16[384,256]{1,0:T(8,128)(2,1)S(1)} %get-tuple-element.42), channel_id=1, source_target_pairs={{0,3},{1,0},{2,1},{3,2},{4,196},{5,197},{6,198},{7,199},{8,11},{9,... | collective-permute-start | bytes 589832 | tf_op jit(solution)/shard_map/ppermute | solution.py:400
  46.0 37.9 %all-to-all-start.1 = ((bf16[64,32,256]{2,1,0:T(8,128)(2,1)}), bf16[64,32,256]{2,1,0:T(8,128)(2,1)S(1)}, u32[]{:S(2)}, u32[]{:S(2)}) async-start(bf16[64,32,256]{2,1,0:T(8,128)(2,1)} %bitcast.2), calls=%async_computation.1 | async-start | bytes 2097152 | tf_op jit(solution)/shard_map/all_to_all | solution.py:405
  56.8 27.1 %copy-start = (bf16[384,2432]{1,0:T(8,128)(2,1)S(1)}, bf16[384,2432]{1,0:T(8,128)(2,1)}, u32[]{:S(2)}) copy-start(bf16[384,2432]{1,0:T(8,128)(2,1)} %get-tuple-element.48.counts_ref) | copy-start | bytes 5603332
  84.6 14.2 %copy-start.1 = (bf16[384,256]{1,0:T(8,128)(2,1)}, bf16[384,256]{1,0:T(8,128)(2,1)S(1)}, u32[]{:S(2)}) copy-start(bf16[384,256]{1,0:T(8,128)(2,1)S(1)} %shard_map.87.refs_3_) | copy-start | bytes 589828
  84.6 8.6 %collective-permute-start.5 = (bf16[384,256]{1,0:T(8,128)(2,1)S(1)}, bf16[384,256]{1,0:T(8,128)(2,1)S(1)}, u32[]{:S(2)}, u32[]{:S(2)}) collective-permute-start(bf16[384,256]{1,0:T(8,128)(2,1)S(1)} %shard_map.87.refs_3_), channel_id=1, source_target_pairs={{0,1},{1,2},{2,3},{3,0},{4,5},{5,6},{6,7},{7,4},{8,9},{9,10},{10,1... | collective-permute-start | bytes 589832 | tf_op jit(solution)/shard_map/ppermute | solution.py:368
  85.6 13.1 %collective-permute-start.4 = (bf16[384,256]{1,0:T(8,128)(2,1)S(1)}, bf16[384,256]{1,0:T(8,128)(2,1)S(1)}, u32[]{:S(2)}, u32[]{:S(2)}) collective-permute-start(bf16[384,256]{1,0:T(8,128)(2,1)S(1)} %shard_map.87.refs_3_), channel_id=1, source_target_pairs={{0,2},{1,3},{2,0},{3,1},{4,6},{5,7},{6,4},{7,5},{8,10},{9,11},{10,... | collective-permute-start | bytes 589832 | tf_op jit(solution)/shard_map/ppermute | solution.py:368
  89.2 9.6 %collective-permute-start.3 = (bf16[384,256]{1,0:T(8,128)(2,1)S(1)}, bf16[384,256]{1,0:T(8,128)(2,1)S(1)}, u32[]{:S(2)}, u32[]{:S(2)}) collective-permute-start(bf16[384,256]{1,0:T(8,128)(2,1)S(1)} %shard_map.87.refs_3_), channel_id=1, source_target_pairs={{0,3},{1,0},{2,1},{3,2},{4,7},{5,4},{6,5},{7,6},{8,11},{9,8},{10,9... | collective-permute-start | bytes 589832 | tf_op jit(solution)/shard_map/ppermute | solution.py:368
  93.3 5.6 %copy-start.2 = (bf16[384,256]{1,0:T(8,128)(2,1)}, bf16[384,256]{1,0:T(8,128)(2,1)S(1)}, u32[]{:S(2)}) copy-start(bf16[384,256]{1,0:T(8,128)(2,1)S(1)} %collective-permute-done.5.refs_6_) | copy-start | bytes 589828
  98.8 0.7 copy-start.3
  98.8 0.7 copy-start.4
  132.5 9.6 %collective-permute-start.6 = (bf16[384,256]{1,0:T(8,128)(2,1)}, bf16[384,256]{1,0:T(8,128)(2,1)S(1)}, u32[]{:S(2)}, u32[]{:S(2)}) collective-permute-start(bf16[384,256]{1,0:T(8,128)(2,1)} %get-tuple-element.52), channel_id=1, source_target_pairs={{0,2},{1,3},{2,0},{3,1},{4,6},{5,7},{6,4},{7,5},{8,10},{9,11},{10,... | collective-permute-start | bytes 589832 | tf_op jit(solution)/shard_map/ppermute | solution.py:368
  134.0 11.5 %collective-permute-start.7 = (bf16[384,256]{1,0:T(8,128)(2,1)}, bf16[384,256]{1,0:T(8,128)(2,1)S(1)}, u32[]{:S(2)}, u32[]{:S(2)}) collective-permute-start(bf16[384,256]{1,0:T(8,128)(2,1)} %get-tuple-element.53), channel_id=1, source_target_pairs={{0,1},{1,2},{2,3},{3,0},{4,5},{5,6},{6,7},{7,4},{8,9},{9,10},{10,1... | collective-permute-start | bytes 589832 | tf_op jit(solution)/shard_map/ppermute | solution.py:368
  136.0 9.5 %collective-permute-start.8 = (bf16[384,256]{1,0:T(8,128)(2,1)}, bf16[384,256]{1,0:T(8,128)(2,1)S(1)}, u32[]{:S(2)}, u32[]{:S(2)}) collective-permute-start(bf16[384,256]{1,0:T(8,128)(2,1)} %get-tuple-element.54), channel_id=1, source_target_pairs={{0,3},{1,0},{2,1},{3,2},{4,7},{5,4},{6,5},{7,6},{8,11},{9,8},{10,9... | collective-permute-start | bytes 589832 | tf_op jit(solution)/shard_map/ppermute | solution.py:368

commit v4 on v3

--- a/solution.py
+++ b/solution.py
@@ -104,41 +104,53 @@
         in_specs=[pl.BlockSpec((parts, others, step, width), lambda i: (0, 0, i, 0))],
         out_specs=[pl.BlockSpec((step, width), lambda i: (i, 0))] * others,
         out_shape=[jax.ShapeDtypeStruct((rows, width), BF16)] * others,
-        compiler_params=pltpu.CompilerParams(vmem_limit_bytes=40 * 2**20),
+        compiler_params=pltpu.CompilerParams(vmem_limit_bytes=20 * 2**20),
     )(terms)
 
 
-def relay_kernel(x_ref, o_ref, wide, place):
+def relay_kernel(x_ref, o_ref, wide, spread, place):
+    lanes = WIDE // 2
+
     @pl.when(pl.program_id(0) == 0)
     def _():
-        row, col = iota((WIDE, WIDE), 0), iota((WIDE, WIDE), 1)
+        row, col = iota((lanes, WIDE), 0), iota((lanes, WIDE), 1)
         for p in range(8):
             keep = (row % NB == col % NB) & (col // NB == p)
-            place[p] = keep.astype(F32).astype(BF16)
-
-    wide[...] = x_ref[0].astype(F32)
-    keep = iota((8, WIDE), 0) == iota((8, WIDE), 1) // NB
-    total = jnp.zeros((WIDE, WIDE), F32)
-    for p in range(8):
-        rows = []
-        for q in range(8):
-            for j in range(4):
-                row = wide[8 * q + p : 8 * q + p + 1, WIDE * j : WIDE * (j + 1)]
-                rows.append(jnp.where(keep, jnp.broadcast_to(row, (8, WIDE)), 0.0))
-        rows = jnp.concatenate(rows, axis=0).astype(BF16)
-        total += jnp.dot(rows, place[p], preferred_element_type=F32)
-    o_ref[0] = total.astype(BF16)
+            place[lanes * p : lanes * (p + 1)] = keep.astype(F32).astype(BF16)
+
+    low = iota((8, lanes), 0) == iota((8, lanes), 1) // NB
+    high = iota((8, lanes), 0) == iota((8, lanes), 1) // NB + 4
+    for a in range(x_ref.shape[0]):
+        wide[a] = x_ref[a].astype(F32)
+        for p in range(8):
+            rows = []
+            for q in range(8):
+                here = slice(8 * q + p, 8 * q + p + 1)
+                for j in range(4):
+                    left = wide[a, here, WIDE * j : WIDE * j + lanes]
+                    right = wide[a, here, WIDE * j + lanes : WIDE * (j + 1)]
+                    left = jnp.broadcast_to(left, (8, lanes))
+                    right = jnp.broadcast_to(right, (8, lanes))
+                    rows.append(jnp.where(low, left, jnp.where(high, right, 0.0)))
+            rows = jnp.concatenate(rows, axis=0).astype(BF16)
+            spread[a, :, lanes * p : lanes * (p + 1)] = rows
+        o_ref[a] = jnp.dot(spread[a], place[...], preferred_element_type=F32).astype(BF16)
 
 
 def relay_coefficients(coefficients):
     atoms, aux, width = coefficients.shape
     return pl.pallas_call(
         relay_kernel,
-        grid=(atoms,),
-        in_specs=[pl.BlockSpec((1, aux, width), lambda i: (i, 0, 0))],
-        out_specs=pl.BlockSpec((1, WIDE, WIDE), lambda i: (i, 0, 0)),
+        grid=(atoms // GROUP,),
+        in_specs=[pl.BlockSpec((GROUP, aux, width), lambda i: (i, 0, 0))],
+        out_specs=pl.BlockSpec((GROUP, WIDE, WIDE), lambda i: (i, 0, 0)),
         out_shape=jax.ShapeDtypeStruct((atoms, WIDE, WIDE), BF16),
-        scratch_shapes=[pltpu.VMEM((aux, width), F32), pltpu.VMEM((8, WIDE, WIDE), BF16)],
+        scratch_shapes=[
+            pltpu.VMEM((GROUP, aux, width), F32),
+            pltpu.VMEM((GROUP, WIDE, 4 * WIDE), BF16),
+            pltpu.VMEM((4 * WIDE, WIDE), BF16),
+        ],
+        compiler_params=pltpu.CompilerParams(vmem_limit_bytes=20 * 2**20),
     )(coefficients)
 
 
@@ -154,13 +166,22 @@
         keep = keep.astype(F32).astype(BF16)
         spread = [jnp.dot(piece, keep, preferred_element_type=F32) for piece in pieces]
         w_ref[:, p, :] = (spread[0] + spread[1]) + spread[2]
-    rows, pool = s_ref.shape
-    lane = iota((rows, pool), 1)
-    total = jnp.zeros((rows, pool), F32)
+    lanes = 128
+    shape = (src_ref.shape[0], lanes)
+    zero, one = jnp.zeros((), BF16), jnp.ones((), BF16)
+    lane = iota(shape, 1).astype(F32).astype(BF16)
+    blocks, hits = [], []
     for g in range(src_ref.shape[1]):
-        index = jnp.where(g < len_ref[...], src_ref[:, g : g + 1], -1)
-        total += jnp.where(lane == index, 1.0, 0.0)
-    s_ref[...] = total.astype(BF16)
+        index = jnp.where(g < len_ref[...], src_ref[:, g : g + 1], -lanes)
+        blocks.append(jnp.broadcast_to(index >> 7, shape).astype(F32).astype(BF16))
+        within = jnp.broadcast_to(index & (lanes - 1), shape).astype(F32).astype(BF16)
+        hits.append(jnp.where(within == lane, one, zero))
+    for b in range(s_ref.shape[1] // lanes):
+        here = jnp.full(shape, b, F32).astype(BF16)
+        total = jnp.zeros(shape, BF16)
+        for block, hit in zip(blocks, hits):
+            total = total + jnp.where(block == here, hit, zero)
+        s_ref[:, lanes * b : lanes * (b + 1)] = total
 
 
 def entry_counts(source_index, list_length, coulomb, pool):
@@ -208,7 +229,7 @@
             jax.ShapeDtypeStruct(shape, BF16),
             jax.ShapeDtypeStruct((rows.shape[0], shape[1]), BF16),
         ),
-        compiler_params=pltpu.CompilerParams(vmem_limit_bytes=40 * 2**20),
+        compiler_params=pltpu.CompilerParams(vmem_limit_bytes=12 * 2**20),
     )(rows, *parts)
 
 
@@ -223,7 +244,7 @@
     return pl.pallas_call(
         list_kernel,
         out_shape=jax.ShapeDtypeStruct((counts.shape[0], slab.shape[1]), BF16),
-        compiler_params=pltpu.CompilerParams(vmem_limit_bytes=40 * 2**20),
+        compiler_params=pltpu.CompilerParams(vmem_limit_bytes=12 * 2**20),
     )(counts, slab, got)
 
 
@@ -250,8 +271,8 @@
     spread = (targets, 8, lanes)
     low = iota(spread, 2) // NB == iota(spread, 1)
     high = iota(spread, 2) // NB + 4 == iota(spread, 1)
-    for r, y_ref in enumerate(y_refs):
-        y_all[(me + r) & 3] = y_ref[...].astype(F32)
+    for ahead, y_ref in zip((0, 1, 3, 2), y_refs):
+        y_all[(me + ahead) & 3] = y_ref[...].astype(F32)
     parts = []
     for j in range(QUARTERS):
         y = y_all[j]
@@ -407,7 +428,7 @@
         got, coeff = lax.optimization_barrier((got, coeff))
         y = list_sums(counts, slab, got.reshape(slots, WIDE))
         far, right, left = along_aux(y, 2), along_aux(y, -1), along_aux(y, 1)
-        own, a, b, c = exchange(aux.reshape(1).astype(jnp.int32), coeff, weights, (y, right, far, left))
+        own, a, b, c = exchange(aux.reshape(1).astype(jnp.int32), coeff, weights, (y, right, left, far))
         total = own.astype(F32) + along_aux(b, 2).astype(F32)
         total += along_aux(a, 1).astype(F32) + along_aux(c, 3).astype(F32)
         return total.astype(BF16)

time: 150 us -> 148 us (0.987); the launches traced: 147 us -> 147 us
  Pallas kernels: 80.9 us -> 63.4 us
  waiting for transfers between devices: 29.3 us -> 41.8 us
  local copies, waits for them, and re-layouts: 3.7 us -> 7.78 us
    pallas_call x1, Pallas kernels: 24.4 us -> 8.59 us  [relay_coefficients(): pl.pallas_call(relay_kernel, grid=(atoms // GROUP,), in_specs=[pl.BlockSp...]
    all_to_all x1, waiting for transfers between devices: 2.77 us -> 14.4 us  [shards(): lax.all_to_all(sent, ('ka', 'pair'), split_axis=0, concat_axis=0, tiled=T...]
    unnamed x18 -> x22, local copies, waits for them, and re-layouts: 0.77 us -> 4.86 us
    all_to_all x1, waiting for transfers between devices: 4.89 us -> 6.64 us  [shards(): lax.all_to_all(terms, AXES, split_axis=0, concat_axis=0, tiled=True, axis...]
    pallas_call x1, Pallas kernels: 13.2 us -> 11.4 us  [entry_counts(): pl.pallas_call(count_kernel, grid=(targets // step,), in_specs=[pl.BlockS...]
  transfers between devices with their start and end apart: 11 -> 11, of which waited for: 8 -> 9; matrix products, arithmetic and copies ran while one was open for 2% -> 2% of each run, Pallas kernels for 26% -> 14%
where the time goes in v4:
time: 148 us; the launch traced here: 147 us
  Pallas kernels  63.4 us (43%)
  waiting for transfers between devices  41.8 us (28%)
  starting transfers between devices  32 us (22%)
  local copies, waits for them, and re-layouts  7.78 us (5%)
  other arithmetic  1.71 us (1%)
    pallas_call x1, Pallas kernels, exchange(): pl.pallas_call(kernel, grid=(atoms // GROUP,), in_specs=[pl.BlockSpec(mem...  33 us
    ppermute x6, waiting for transfers between devices, along_aux(): lax.ppermute(array, 'aux', [(i, (i + by) % QUARTERS) for i in range(QUART...  17 us
    all_to_all x1, waiting for transfers between devices, shards(): lax.all_to_all(sent, ('ka', 'pair'), split_axis=0, concat_axis=0, tiled=T...  14.4 us
    pallas_call x1, Pallas kernels, entry_counts(): pl.pallas_call(count_kernel, grid=(targets // step,), in_specs=[pl.BlockS...  11.4 us
    all_to_all x1, starting transfers between devices, shards(): lax.all_to_all(sent, ('ka', 'pair'), split_axis=0, concat_axis=0, tiled=T...  10.8 us
    ppermute x6, starting transfers between devices, along_aux(): lax.ppermute(array, 'aux', [(i, (i + by) % QUARTERS) for i in range(QUART...  9.83 us
    pallas_call x1, Pallas kernels, relay_coefficients(): pl.pallas_call(relay_kernel, grid=(atoms // GROUP,), in_specs=[pl.BlockSp...  8.59 us
    all_to_all x1, waiting for transfers between devices, shards(): lax.all_to_all(terms, AXES, split_axis=0, concat_axis=0, tiled=True, axis...  6.64 us
  transfers between devices with their start and end apart: 11, of which 9 were waited for; matrix products, arithmetic and copies ran while one was open for 2% of the time, Pallas kernels for 14%

profile of v4, /device:TPU:2, one launch (start us, length us, event | category | flops | bytes accessed | tf_op | source)
XLA Modules:
  0.0 146.9 jit_solution(8432404372627137870)
XLA Ops:
  0.0 6.5 %shard_map.82 = bf16[4,4,384,256]{3,2,1,0:T(8,128)(2,1)} custom-call(s32[1,3]{1,0:T(1,128)} %kp_ref.1, s32[3,4,384]{2,1,0:T(4,128)} %shift_ref.1, bf16[1536,2,1024]{2,1,0:T(2,128)(2,1)} %bitcast.5), custom_call_target="tpu_custom_call" | custom-call | tf_op jit(solution)/shard_map/pallas_call | solution.py:75
  6.5 0.0 copy-start.9
  6.5 0.0 copy-start.8
  6.5 0.0 copy-start.10
  6.5 0.0 copy-start.7
  6.5 6.1 %all-to-all-start = ((bf16[4,4,384,256]{3,2,1,0:T(8,128)(2,1)}), bf16[4,4,384,256]{3,2,1,0:T(8,128)(2,1)S(1)}, u32[]{:S(2)}, u32[]{:S(2)}) async-start(bf16[4,4,384,256]{3,2,1,0:T(8,128)(2,1)} %shard_map.82), calls=%async_computation | async-start | bytes 6291456 | tf_op jit(solution)/shard_map/all_to_all | solution.py:411
  12.6 0.0 copy-done.9
  12.6 0.1 copy.15
  12.7 0.1 reshape.13
  12.8 0.8 copy.12.src_ref
  13.6 0.8 broadcast_in_dim.4.len_ref
  14.4 0.8 copy.14.coul_ref
  15.2 11.4 %shard_map.83 = (bf16[384,2432]{1,0:T(8,128)(2,1)}, f32[384,8,256]{2,1,0:T(8,128)}) custom-call(s32[384,16]{1,0:T(8,128)} %copy.12.src_ref, s32[384,1]{1,0:T(8,128)} %broadcast_in_dim.4.len_ref, f32[384,64]{1,0:T(8,128)} %copy.14.coul_ref), custom_call_target="tpu_custom_call" | custom-call | tf_op jit(solution)/shard_map/pallas_call | solution.py:191
  26.6 6.6 %all-to-all-done.x_ref = bf16[4,4,384,256]{3,2,1,0:T(8,128)(2,1)S(1)} async-done(((bf16[4,4,384,256]{3,2,1,0:T(8,128)(2,1)}), bf16[4,4,384,256]{3,2,1,0:T(8,128)(2,1)S(1)}, u32[]{:S(2)}, u32[]{:S(2)}) %all-to-all-start) | async-done | bytes 3145760 | tf_op jit(solution)/shard_map/all_to_all | solution.py:411
  33.3 1.5 %shard_map.84 = (bf16[384,256]{1,0:T(8,128)(2,1)S(1)}, bf16[384,256]{1,0:T(8,128)(2,1)}, bf16[384,256]{1,0:T(8,128)(2,1)}, bf16[384,256]{1,0:T(8,128)(2,1)S(1)}) custom-call(bf16[4,4,384,256]{3,2,1,0:T(8,128)(2,1)S(1)} %all-to-all-done.x_ref), custom_call_target="tpu_custom_call" | custom-call | tf_op jit(solution)/shard_map/pallas_call | solution.py:101
  34.8 2.1 %collective-permute-start = (bf16[384,256]{1,0:T(8,128)(2,1)}, bf16[384,256]{1,0:T(8,128)(2,1)S(1)}, u32[]{:S(2)}, u32[]{:S(2)}) collective-permute-start(bf16[384,256]{1,0:T(8,128)(2,1)} %get-tuple-element.40), channel_id=1, source_target_pairs={{0,2},{1,3},{2,0},{3,1},{4,132},{5,133},{6,134},{7,135},{8,10},{9,... | collective-permute-start | bytes 589832 | tf_op jit(solution)/shard_map/ppermute | solution.py:421
  36.9 0.7 collective-permute-start.1
  37.6 2.6 %collective-permute-start.2 = (bf16[384,256]{1,0:T(8,128)(2,1)S(1)}, bf16[384,256]{1,0:T(8,128)(2,1)S(1)}, u32[]{:S(2)}, u32[]{:S(2)}) collective-permute-start(bf16[384,256]{1,0:T(8,128)(2,1)S(1)} %get-tuple-element.42), channel_id=1, source_target_pairs={{0,3},{1,0},{2,1},{3,2},{4,196},{5,197},{6,198},{7,199},{8,11},{9,... | collective-permute-start | bytes 589832 | tf_op jit(solution)/shard_map/ppermute | solution.py:421
  40.2 0.4 copy.16.rows_ref
  40.5 1.7 %collective-permute-done.a_ref = bf16[384,256]{1,0:T(8,128)(2,1)S(1)} collective-permute-done((bf16[384,256]{1,0:T(8,128)(2,1)}, bf16[384,256]{1,0:T(8,128)(2,1)S(1)}, u32[]{:S(2)}, u32[]{:S(2)}) %collective-permute-start) | collective-permute-done | bytes 196640 | tf_op jit(solution)/shard_map/ppermute | solution.py:421
  42.2 2.1 %collective-permute-done.1.b_ref = bf16[384,256]{1,0:T(8,128)(2,1)S(1)} collective-permute-done((bf16[384,256]{1,0:T(8,128)(2,1)}, bf16[384,256]{1,0:T(8,128)(2,1)S(1)}, u32[]{:S(2)}, u32[]{:S(2)}) %collective-permute-start.1) | collective-permute-done | bytes 196640 | tf_op jit(solution)/shard_map/ppermute | solution.py:421
  44.3 0.0 collective-permute-done.2.c_ref
  44.3 1.7 %shard_map.85 = (bf16[384,256]{1,0:T(8,128)(2,1)S(1)}, bf16[2048,256]{1,0:T(8,128)(2,1)}) custom-call(s32[2048,1]{1,0:T(8,128)S(1)} %copy.16.rows_ref, bf16[384,256]{1,0:T(8,128)(2,1)S(1)} %get-tuple-element.39.own_ref, bf16[384,256]{1,0:T(8,128)(2,1)S(1)} %collective-permute-done.a_ref, bf16[384,256]{1,0:T(8,128)(2,1)S(1)} %collective-permute-done.1.b_ref, ...), custom_call_target="tpu_custom_call" | custom-call | tf_op jit(solution)/shard_map/pallas_call | solution.py:226
  46.0 10.8 %all-to-all-start.1 = ((bf16[64,32,256]{2,1,0:T(8,128)(2,1)}), bf16[64,32,256]{2,1,0:T(8,128)(2,1)S(1)}, u32[]{:S(2)}, u32[]{:S(2)}) async-start(bf16[64,32,256]{2,1,0:T(8,128)(2,1)} %bitcast.2), calls=%async_computation.1 | async-start | bytes 2097152 | tf_op jit(solution)/shard_map/all_to_all | solution.py:426
  56.8 0.0 copy-start.1
  56.9 2.2 %copy-done.1 = bf16[32,64,1024]{2,1,0:T(8,128)(2,1)S(1)} copy-done((bf16[32,64,1024]{2,1,0:T(8,128)(2,1)S(1)}, bf16[32,64,1024]{2,1,0:T(8,128)(2,1)}, u32[]{:S(2)}) %copy-start.1) | copy-done | bytes 4194328
  59.0 8.6 %shard_map.86.refs_1_ = bf16[32,256,256]{2,1,0:T(8,128)(2,1)S(1)} custom-call(bf16[32,64,1024]{2,1,0:T(8,128)(2,1)S(1)} %copy-done.1), custom_call_target="tpu_custom_call" | custom-call | tf_op jit(solution)/shard_map/pallas_call | solution.py:142
  67.6 0.0 copy-start
  67.6 1.9 %copy-done = bf16[32,256,256]{2,1,0:T(8,128)(2,1)} copy-done((bf16[32,256,256]{2,1,0:T(8,128)(2,1)}, bf16[32,256,256]{2,1,0:T(8,128)(2,1)S(1)}, u32[]{:S(2)}) %copy-start) | copy-done | bytes 4194328
  69.6 14.4 %all-to-all-done.1 = bf16[64,32,256]{2,1,0:T(8,128)(2,1)S(1)} async-done(((bf16[64,32,256]{2,1,0:T(8,128)(2,1)}), bf16[64,32,256]{2,1,0:T(8,128)(2,1)S(1)}, u32[]{:S(2)}, u32[]{:S(2)}) %all-to-all-start.1) | async-done | bytes 1048608 | tf_op jit(solution)/shard_map/all_to_all | solution.py:426
  84.0 0.7 shard_map.87.refs_3_
  84.7 0.0 copy-start.3
  84.7 1.7 %collective-permute-start.5 = (bf16[384,256]{1,0:T(8,128)(2,1)S(1)}, bf16[384,256]{1,0:T(8,128)(2,1)S(1)}, u32[]{:S(2)}, u32[]{:S(2)}) collective-permute-start(bf16[384,256]{1,0:T(8,128)(2,1)S(1)} %shard_map.87.refs_3_), channel_id=1, source_target_pairs={{0,2},{1,3},{2,0},{3,1},{4,6},{5,7},{6,4},{7,5},{8,10},{9,11},{10,... | collective-permute-start | bytes 589832 | tf_op jit(solution)/shard_map/ppermute | solution.py:389
  86.3 2.3 %collective-permute-start.4 = (bf16[384,256]{1,0:T(8,128)(2,1)S(1)}, bf16[384,256]{1,0:T(8,128)(2,1)S(1)}, u32[]{:S(2)}, u32[]{:S(2)}) collective-permute-start(bf16[384,256]{1,0:T(8,128)(2,1)S(1)} %shard_map.87.refs_3_), channel_id=1, source_target_pairs={{0,1},{1,2},{2,3},{3,0},{4,5},{5,6},{6,7},{7,4},{8,9},{9,10},{10,1... | collective-permute-start | bytes 589832 | tf_op jit(solution)/shard_map/ppermute | solution.py:389
  88.6 1.0 collective-permute-start.3
  89.6 4.2 %collective-permute-done.5.refs_6_ = bf16[384,256]{1,0:T(8,128)(2,1)S(1)} collective-permute-done((bf16[384,256]{1,0:T(8,128)(2,1)S(1)}, bf16[384,256]{1,0:T(8,128)(2,1)S(1)}, u32[]{:S(2)}, u32[]{:S(2)}) %collective-permute-start.5) | collective-permute-done | bytes 196640 | tf_op jit(solution)/shard_map/ppermute | solution.py:389
  93.8 4.5 %collective-permute-done.4.refs_5_ = bf16[384,256]{1,0:T(8,128)(2,1)S(1)} collective-permute-done((bf16[384,256]{1,0:T(8,128)(2,1)S(1)}, bf16[384,256]{1,0:T(8,128)(2,1)S(1)}, u32[]{:S(2)}, u32[]{:S(2)}) %collective-permute-start.4) | collective-permute-done | bytes 196640 | tf_op jit(solution)/shard_map/ppermute | solution.py:389
  98.2 0.0 collective-permute-done.3.refs_4_
  98.3 0.6 copy-done.5
  98.9 0.1 copy-done.6
  99.0 33.0 %shard_map.88 = (bf16[384,256]{1,0:T(8,128)(2,1)}, bf16[384,256]{1,0:T(8,128)(2,1)}, bf16[384,256]{1,0:T(8,128)(2,1)}, bf16[384,256]{1,0:T(8,128)(2,1)}) custom-call(s32[1]{0:T(128)} %bitcast.refs_0_, bf16[32,256,256]{2,1,0:T(8,128)(2,1)} %copy-done, f32[384,8,256]{2,1,0:T(8,128)} %get-tuple-element.47.refs_2_, bf16[384,256]{1,0:T(8,128)(2,1)} %copy-done.3, ...), custom_call_target="tpu_custom_call" | custom-call | tf_op jit(solution)/shard_map/pallas_call | solution.py:338
  132.0 1.7 %collective-permute-start.6 = (bf16[384,256]{1,0:T(8,128)(2,1)}, bf16[384,256]{1,0:T(8,128)(2,1)S(1)}, u32[]{:S(2)}, u32[]{:S(2)}) collective-permute-start(bf16[384,256]{1,0:T(8,128)(2,1)} %get-tuple-element.52), channel_id=1, source_target_pairs={{0,2},{1,3},{2,0},{3,1},{4,6},{5,7},{6,4},{7,5},{8,10},{9,11},{10,... | collective-permute-start | bytes 589832 | tf_op jit(solution)/shard_map/ppermute | solution.py:389
  133.7 2.2 %collective-permute-start.7 = (bf16[384,256]{1,0:T(8,128)(2,1)}, bf16[384,256]{1,0:T(8,128)(2,1)S(1)}, u32[]{:S(2)}, u32[]{:S(2)}) collective-permute-start(bf16[384,256]{1,0:T(8,128)(2,1)} %get-tuple-element.53), channel_id=1, source_target_pairs={{0,1},{1,2},{2,3},{3,0},{4,5},{5,6},{6,7},{7,4},{8,9},{9,10},{10,1... | collective-permute-start | bytes 589832 | tf_op jit(solution)/shard_map/ppermute | solution.py:389
  135.9 1.0 collective-permute-start.8
  136.9 4.7 %collective-permute-done.6 = bf16[384,256]{1,0:T(8,128)(2,1)S(1)} collective-permute-done((bf16[384,256]{1,0:T(8,128)(2,1)}, bf16[384,256]{1,0:T(8,128)(2,1)S(1)}, u32[]{:S(2)}, u32[]{:S(2)}) %collective-permute-start.6) | collective-permute-done | bytes 196640 | tf_op jit(solution)/shard_map/ppermute | solution.py:389
  141.6 3.4 %collective-permute-done.7 = bf16[384,256]{1,0:T(8,128)(2,1)S(1)} collective-permute-done((bf16[384,256]{1,0:T(8,128)(2,1)}, bf16[384,256]{1,0:T(8,128)(2,1)S(1)}, u32[]{:S(2)}, u32[]{:S(2)}) %collective-permute-start.7) | collective-permute-done | bytes 196640 | tf_op jit(solution)/shard_map/ppermute | solution.py:389
  144.9 0.3 collective-permute-done.8
  145.2 1.7 %add_convert_fusion = bf16[384,256]{1,0:T(8,128)(2,1)} fusion(bf16[384,256]{1,0:T(8,128)(2,1)S(1)} %collective-permute-done.8, bf16[384,256]{1,0:T(8,128)(2,1)S(1)} %collective-permute-done.7, bf16[384,256]{1,0:T(8,128)(2,1)S(1)} %collective-permute-done.6, bf16[384,256]{1,0:T(8,128)(2,1)} %get-tuple-element.51), kind=kLoop, calls=%fused_computation | loop fusion | flops 786432 | bytes 983040 | tf_op jit(solution)/shard_map/convert_element_type | solution.py:434
  (10 shorter events, 0.0 us)
Async XLA Ops:
  6.5 6.1 %copy-start.9 = (s32[1,64,32]{1,2,0:T(8,128)S(1)}, s32[1,64,32]{1,2,0:T(8,128)}, u32[]{:S(2)}) copy-start(s32[1,64,32]{1,2,0:T(8,128)} %param.13) | copy-start | bytes 24580
  6.5 6.3 %copy-start.8 = (s32[384,16]{0,1:T(8,128)S(1)}, s32[384,16]{0,1:T(8,128)}, u32[]{:S(2)}) copy-start(s32[384,16]{0,1:T(8,128)} %param.14) | copy-start | bytes 73732
  6.5 7.1 %copy-start.10 = (s32[384]{0:T(512)S(1)}, s32[384]{0:T(512)}, u32[]{:S(2)}) copy-start(s32[384]{0:T(512)} %param.15) | copy-start | bytes 4612
  6.5 7.9 %copy-start.7 = (f32[384,64]{0,1:T(8,128)S(1)}, f32[384,64]{0,1:T(8,128)}, u32[]{:S(2)}) copy-start(f32[384,64]{0,1:T(8,128)} %param.12) | copy-start | bytes 294916
  6.5 26.8 %all-to-all-start = ((bf16[4,4,384,256]{3,2,1,0:T(8,128)(2,1)}), bf16[4,4,384,256]{3,2,1,0:T(8,128)(2,1)S(1)}, u32[]{:S(2)}, u32[]{:S(2)}) async-start(bf16[4,4,384,256]{3,2,1,0:T(8,128)(2,1)} %shard_map.82), calls=%async_computation | async-start | bytes 6291456 | tf_op jit(solution)/shard_map/all_to_all | solution.py:411
  34.8 7.4 %collective-permute-start = (bf16[384,256]{1,0:T(8,128)(2,1)}, bf16[384,256]{1,0:T(8,128)(2,1)S(1)}, u32[]{:S(2)}, u32[]{:S(2)}) collective-permute-start(bf16[384,256]{1,0:T(8,128)(2,1)} %get-tuple-element.40), channel_id=1, source_target_pairs={{0,2},{1,3},{2,0},{3,1},{4,132},{5,133},{6,134},{7,135},{8,10},{9,... | collective-permute-start | bytes 589832 | tf_op jit(solution)/shard_map/ppermute | solution.py:421
  36.9 7.4 %collective-permute-start.1 = (bf16[384,256]{1,0:T(8,128)(2,1)}, bf16[384,256]{1,0:T(8,128)(2,1)S(1)}, u32[]{:S(2)}, u32[]{:S(2)}) collective-permute-start(bf16[384,256]{1,0:T(8,128)(2,1)} %get-tuple-element.41), channel_id=1, source_target_pairs={{0,1},{1,2},{2,3},{3,0},{4,68},{5,69},{6,70},{7,71},{8,9},{9,10},{... | collective-permute-start | bytes 589832 | tf_op jit(solution)/shard_map/ppermute | solution.py:421
  37.6 6.7 %collective-permute-start.2 = (bf16[384,256]{1,0:T(8,128)(2,1)S(1)}, bf16[384,256]{1,0:T(8,128)(2,1)S(1)}, u32[]{:S(2)}, u32[]{:S(2)}) collective-permute-start(bf16[384,256]{1,0:T(8,128)(2,1)S(1)} %get-tuple-element.42), channel_id=1, source_target_pairs={{0,3},{1,0},{2,1},{3,2},{4,196},{5,197},{6,198},{7,199},{8,11},{9,... | collective-permute-start | bytes 589832 | tf_op jit(solution)/shard_map/ppermute | solution.py:421
  46.0 37.9 %all-to-all-start.1 = ((bf16[64,32,256]{2,1,0:T(8,128)(2,1)}), bf16[64,32,256]{2,1,0:T(8,128)(2,1)S(1)}, u32[]{:S(2)}, u32[]{:S(2)}) async-start(bf16[64,32,256]{2,1,0:T(8,128)(2,1)} %bitcast.2), calls=%async_computation.1 | async-start | bytes 2097152 | tf_op jit(solution)/shard_map/all_to_all | solution.py:426
  56.8 2.2 %copy-start.1 = (bf16[32,64,1024]{2,1,0:T(8,128)(2,1)S(1)}, bf16[32,64,1024]{2,1,0:T(8,128)(2,1)}, u32[]{:S(2)}) copy-start(bf16[32,64,1024]{2,1,0:T(8,128)(2,1)} %x_ref) | copy-start | bytes 12582916
  59.0 24.9 %copy-start.2 = (bf16[384,2432]{1,0:T(8,128)(2,1)S(1)}, bf16[384,2432]{1,0:T(8,128)(2,1)}, u32[]{:S(2)}) copy-start(bf16[384,2432]{1,0:T(8,128)(2,1)} %get-tuple-element.48.counts_ref) | copy-start | bytes 5603332
  67.6 2.0 %copy-start = (bf16[32,256,256]{2,1,0:T(8,128)(2,1)}, bf16[32,256,256]{2,1,0:T(8,128)(2,1)S(1)}, u32[]{:S(2)}) copy-start(bf16[32,256,256]{2,1,0:T(8,128)(2,1)S(1)} %shard_map.86.refs_1_) | copy-start | bytes 12582916
  84.7 13.6 %copy-start.3 = (bf16[384,256]{1,0:T(8,128)(2,1)}, bf16[384,256]{1,0:T(8,128)(2,1)S(1)}, u32[]{:S(2)}) copy-start(bf16[384,256]{1,0:T(8,128)(2,1)S(1)} %shard_map.87.refs_3_) | copy-start | bytes 589828
  84.7 9.1 %collective-permute-start.5 = (bf16[384,256]{1,0:T(8,128)(2,1)S(1)}, bf16[384,256]{1,0:T(8,128)(2,1)S(1)}, u32[]{:S(2)}, u32[]{:S(2)}) collective-permute-start(bf16[384,256]{1,0:T(8,128)(2,1)S(1)} %shard_map.87.refs_3_), channel_id=1, source_target_pairs={{0,2},{1,3},{2,0},{3,1},{4,6},{5,7},{6,4},{7,5},{8,10},{9,11},{10,... | collective-permute-start | bytes 589832 | tf_op jit(solution)/shard_map/ppermute | solution.py:389
  86.3 11.9 %collective-permute-start.4 = (bf16[384,256]{1,0:T(8,128)(2,1)S(1)}, bf16[384,256]{1,0:T(8,128)(2,1)S(1)}, u32[]{:S(2)}, u32[]{:S(2)}) collective-permute-start(bf16[384,256]{1,0:T(8,128)(2,1)S(1)} %shard_map.87.refs_3_), channel_id=1, source_target_pairs={{0,1},{1,2},{2,3},{3,0},{4,5},{5,6},{6,7},{7,4},{8,9},{9,10},{10,1... | collective-permute-start | bytes 589832 | tf_op jit(solution)/shard_map/ppermute | solution.py:389
  88.6 9.6 %collective-permute-start.3 = (bf16[384,256]{1,0:T(8,128)(2,1)S(1)}, bf16[384,256]{1,0:T(8,128)(2,1)S(1)}, u32[]{:S(2)}, u32[]{:S(2)}) collective-permute-start(bf16[384,256]{1,0:T(8,128)(2,1)S(1)} %shard_map.87.refs_3_), channel_id=1, source_target_pairs={{0,3},{1,0},{2,1},{3,2},{4,7},{5,4},{6,5},{7,6},{8,11},{9,8},{10,9... | collective-permute-start | bytes 589832 | tf_op jit(solution)/shard_map/ppermute | solution.py:389
  93.8 4.5 %copy-start.4 = (bf16[384,256]{1,0:T(8,128)(2,1)}, bf16[384,256]{1,0:T(8,128)(2,1)S(1)}, u32[]{:S(2)}) copy-start(bf16[384,256]{1,0:T(8,128)(2,1)S(1)} %collective-permute-done.5.refs_6_) | copy-start | bytes 589828
  98.2 0.7 copy-start.5
  98.3 0.7 copy-start.6
  132.0 9.6 %collective-permute-start.6 = (bf16[384,256]{1,0:T(8,128)(2,1)}, bf16[384,256]{1,0:T(8,128)(2,1)S(1)}, u32[]{:S(2)}, u32[]{:S(2)}) collective-permute-start(bf16[384,256]{1,0:T(8,128)(2,1)} %get-tuple-element.52), channel_id=1, source_target_pairs={{0,2},{1,3},{2,0},{3,1},{4,6},{5,7},{6,4},{7,5},{8,10},{9,11},{10,... | collective-permute-start | bytes 589832 | tf_op jit(solution)/shard_map/ppermute | solution.py:389
  133.7 11.3 %collective-permute-start.7 = (bf16[384,256]{1,0:T(8,128)(2,1)}, bf16[384,256]{1,0:T(8,128)(2,1)S(1)}, u32[]{:S(2)}, u32[]{:S(2)}) collective-permute-start(bf16[384,256]{1,0:T(8,128)(2,1)} %get-tuple-element.53), channel_id=1, source_target_pairs={{0,1},{1,2},{2,3},{3,0},{4,5},{5,6},{6,7},{7,4},{8,9},{9,10},{10,1... | collective-permute-start | bytes 589832 | tf_op jit(solution)/shard_map/ppermute | solution.py:389
  135.9 9.3 %collective-permute-start.8 = (bf16[384,256]{1,0:T(8,128)(2,1)}, bf16[384,256]{1,0:T(8,128)(2,1)S(1)}, u32[]{:S(2)}, u32[]{:S(2)}) collective-permute-start(bf16[384,256]{1,0:T(8,128)(2,1)} %get-tuple-element.54), channel_id=1, source_target_pairs={{0,3},{1,0},{2,1},{3,2},{4,7},{5,4},{6,5},{7,6},{8,11},{9,8},{10,9... | collective-permute-start | bytes 589832 | tf_op jit(solution)/shard_map/ppermute | solution.py:389
